TPU v7x, 32 devices: a whole 2x2x4 slice. The times are simulated.
32 devices in a mesh: dp: 4 (over z), expert: 4 (over y, core), etensor: 2 (over x).
Axes of the slice: x: 2, y: 2, z: 4, core: 2. Of those that a mesh axis runs over, the one named last changes fastest.
Arguments:
- token_rows: bfloat16 [2048, 4096], P(('dp', 'expert')), may hold values from -6 to 6
- row_grads: bfloat16 [2048, 4096], P(('dp', 'expert')), may hold values from -6 to 6
- gate_scale: bfloat16 [2048], P(('dp', 'expert')), may hold values from 0.099609375 to 1
- routing: int32 [2048, 1], P(('dp', 'expert')), may hold values from 0 to 3; in each aligned block of 128 rows (0 to 127, 128 to 255, ...) at most 48 rows name the same one
- gate_weight: bfloat16 [4, 14336, 4096], P('expert', ('dp', 'etensor')), may hold values from -0.09375 to 0.09375
- up_weight: bfloat16 [4, 14336, 4096], P('expert', ('dp', 'etensor')), may hold values from -0.09375 to 0.09375
- down_weight: bfloat16 [4, 14336, 4096], P('expert', ('dp', 'etensor')), may hold values from -0.046875 to 0.046875
Outputs:
- input_grads: bfloat16 [2048, 4096], P(('dp', 'expert'))
- scale_grads: float32 [2048], P(('dp', 'expert'))
- grad_gate_weight: bfloat16 [4, 14336, 4096], P('expert', ('dp', 'etensor'))
- grad_up_weight: bfloat16 [4, 14336, 4096], P('expert', ('dp', 'etensor'))
- grad_down_weight: bfloat16 [4, 14336, 4096], P('expert', ('dp', 'etensor'))
Inputs may be any that keep to these rules, and one draw needn't show every extreme that they name: `routing`: among the 128 rows of one aligned block (the rows of one index of dp and expert) no expert is named more than 48 times.
All inputs are finite; a program needn't handle non-finite values.
Results may differ from a plain program's by a relative error of at most 0.0057.
Values may be sent and summed in bfloat16 or wider, within the bound.
No kernel may reach another device: no remote copies, remote signals or barrier semaphores. Data moves between devices by JAX's collectives and lax.ppermute only.
A program may use at most 256 MiB of HBM per device.

v0:
```python
import jax
import jax.numpy as jnp
from jax import lax
from jax.sharding import PartitionSpec as P


def per_device(token_rows, row_grads, gate_scale, routing, gate_weight, up_weight, down_weight):
    experts = lax.axis_size("expert")
    width = token_rows.shape[1]
    local_rows = token_rows.shape[0]
    capacity = 3 * local_rows // 8
    route = routing[:, 0]
    hits = (route[:, None] == jnp.arange(experts, dtype=jnp.int32)[None, :]).astype(jnp.int32)
    before = jnp.cumsum(hits, axis=0) - hits
    slot_pos = route * capacity + jnp.sum(before * hits, axis=1)
    placing = (
        jnp.arange(experts * capacity, dtype=jnp.int32)[:, None] == slot_pos[None, :]
    ).astype(jnp.bfloat16)
    send_rows = (
        jnp.dot(placing, token_rows, preferred_element_type=jnp.float32)
        .astype(jnp.bfloat16)
        .reshape(experts, capacity, width)
    )
    send_grads = (
        jnp.dot(placing, row_grads, preferred_element_type=jnp.float32)
        .astype(jnp.bfloat16)
        .reshape(experts, capacity, width)
    )
    send_scale = (
        jnp.dot(placing, gate_scale, preferred_element_type=jnp.float32)
        .astype(jnp.bfloat16)
        .reshape(experts, capacity)
    )
    recv_rows, recv_grads, recv_scale = (
        lax.all_to_all(send_rows, "expert", split_axis=0, concat_axis=0, tiled=True),
        lax.all_to_all(send_grads, "expert", split_axis=0, concat_axis=0, tiled=True),
        lax.all_to_all(send_scale, "expert", split_axis=0, concat_axis=0, tiled=True),
    )
    group_rows, group_grads, group_scale = (
        lax.all_gather(recv_rows.reshape(-1, width), "dp", axis=0, tiled=True),
        lax.all_gather(recv_grads.reshape(-1, width), "dp", axis=0, tiled=True),
        lax.all_gather(recv_scale.reshape(-1), "dp", axis=0, tiled=True),
    )
    w_gate = gate_weight[0]
    w_up = up_weight[0]
    w_down = down_weight[0]
    scale_column = group_scale.astype(jnp.float32)[:, None]
    gate_pre = jnp.einsum("rd,fd->rf", group_rows, w_gate, preferred_element_type=jnp.float32)
    up_pre = jnp.einsum("rd,fd->rf", group_rows, w_up, preferred_element_type=jnp.float32)
    sigmoid_gate = jax.nn.sigmoid(gate_pre)
    activated = gate_pre * sigmoid_gate
    hidden = (activated * up_pre).astype(jnp.bfloat16)
    hidden_raw = jnp.einsum("rd,fd->rf", group_grads, w_down, preferred_element_type=jnp.float32)
    scale_term = jnp.sum(hidden.astype(jnp.float32) * hidden_raw, axis=1)
    hidden_grad = scale_column * hidden_raw
    gate_pre_grad = (
        hidden_grad * up_pre * sigmoid_gate * (1.0 + gate_pre * (1.0 - sigmoid_gate))
    ).astype(jnp.bfloat16)
    up_pre_grad = (hidden_grad * activated).astype(jnp.bfloat16)
    scaled_grads = (scale_column * group_grads.astype(jnp.float32)).astype(jnp.bfloat16)
    grad_gate = jnp.einsum(
        "rf,rd->fd", gate_pre_grad, group_rows, preferred_element_type=jnp.float32
    ).astype(jnp.bfloat16)
    grad_up = jnp.einsum(
        "rf,rd->fd", up_pre_grad, group_rows, preferred_element_type=jnp.float32
    ).astype(jnp.bfloat16)
    grad_down = jnp.einsum(
        "rf,rd->fd", hidden, scaled_grads, preferred_element_type=jnp.float32
    ).astype(jnp.bfloat16)
    row_term = jnp.dot(gate_pre_grad, w_gate, preferred_element_type=jnp.float32) + jnp.dot(
        up_pre_grad, w_up, preferred_element_type=jnp.float32
    )
    share_total, share_scale = (
        lax.psum_scatter(row_term, ("dp", "etensor"), scatter_dimension=0, tiled=True),
        lax.psum_scatter(scale_term, ("dp", "etensor"), scatter_dimension=0, tiled=True),
    )
    row_total, scale_total = (
        lax.all_gather(share_total, "etensor", axis=0, tiled=True),
        lax.all_gather(share_scale, "etensor", axis=0, tiled=True),
    )
    back_rows, back_scale = (
        lax.all_to_all(
            row_total.reshape(experts, capacity, width),
            "expert",
            split_axis=0,
            concat_axis=0,
            tiled=True,
        ),
        lax.all_to_all(
            scale_total.reshape(experts, capacity),
            "expert",
            split_axis=0,
            concat_axis=0,
            tiled=True,
        ),
    )
    input_grads = jnp.take(back_rows.reshape(-1, width), slot_pos, axis=0).astype(jnp.bfloat16)
    scale_grads = jnp.take(back_scale.reshape(-1), slot_pos, axis=0)
    return (input_grads, scale_grads, grad_gate[None], grad_up[None], grad_down[None])


def solution(mesh):
    in_specs = (
        P(("dp", "expert"), None),
        P(("dp", "expert"), None),
        P(("dp", "expert")),
        P(("dp", "expert"), None),
        P("expert", ("dp", "etensor"), None),
        P("expert", ("dp", "etensor"), None),
        P("expert", ("dp", "etensor"), None),
    )
    out_specs = (
        P(("dp", "expert"), None),
        P(("dp", "expert")),
        P("expert", ("dp", "etensor"), None),
        P("expert", ("dp", "etensor"), None),
        P("expert", ("dp", "etensor"), None),
    )
    return jax.shard_map(
        per_device, mesh=mesh, in_specs=in_specs, out_specs=out_specs, check_vma=False
    )
```

profile of v0, /device:TPU:0, one launch (start us, length us, event | category | flops | bytes accessed | tf_op | source)
XLA Modules:
  0.0 634.3 jit_solution(12829704623060854638)
XLA Ops:
  7.2 0.0 copy-start
  7.2 0.0 copy-start.2
  7.2 0.0 all-gather.6.cloned.1.call-start
  7.2 0.9 fusion.19
  8.1 0.2 reduce_window_sum.11
  8.3 0.8 select_reduce_fusion
  9.1 0.7 multiply_add_fusion
  9.8 0.0 copy-done
  9.8 0.6 convolution_convert_fusion.3
  10.4 0.0 copy-start.5
  10.4 0.0 copy-start.8
  10.4 24.2 %all_to_all.34 = bf16[4,48,4096]{2,1,0:T(8,128)(2,1)} all-to-all(bf16[4,48,4096]{2,1,0:T(8,128)(2,1)S(1)} %bitcast.62), channel_id=1, replica_groups=mesh['dp'=4,'expert'=4,'etensor'=2] {'expert'}, dimensions={0} | all-to-all | bytes 3145728 | tf_op jit(solution)/shard_map/all_to_all | solution.py:35
  34.6 0.0 all-gather.6.cloned.1.call-update
  34.6 0.0 all-gather.4.cloned.1.call-start
  34.7 0.0 copy-done.2
  34.7 0.6 convolution_convert_fusion.4
  35.3 23.3 %all_to_all.35 = bf16[4,48,4096]{2,1,0:T(8,128)(2,1)} all-to-all(bf16[4,48,4096]{2,1,0:T(8,128)(2,1)S(1)} %bitcast.63), channel_id=1, replica_groups=mesh['dp'=4,'expert'=4,'etensor'=2] {'expert'}, dimensions={0} | all-to-all | bytes 3145728 | tf_op jit(solution)/shard_map/all_to_all | solution.py:36
  58.5 0.0 all-gather.4.cloned.1.call-update
  58.6 0.0 copy-done.5
  58.6 0.1 fusion.18
  58.7 0.7 all_to_all.28
  59.4 3.2 all-to-all-start
  62.6 0.0 reduce-scatter.2.cloned.1.call-start
  62.7 0.0 copy-done.8
  62.7 0.6 dynamic-slice
  64.0 2.3 all-to-all-done
  66.3 0.1 reshape.83
  66.4 0.2 dynamic-update-slice
  66.6 12.9 %all-reduce = bf16[768]{0:T(1024)(128)(2,1)S(1)} all-reduce(bf16[768]{0:T(1024)(128)(2,1)S(1)} %dynamic-update-slice), channel_id=1, replica_groups=mesh['dp'=4,'expert'=4,'etensor'=2] {'dp'}, use_global_device_ids=true, to_apply=%add | all-reduce | flops 768 | bytes 3072
  79.5 71.7 %all-gather.6.cloned.1.call-done = bf16[768,4096]{1,0:T(8,128)(2,1)} async-done(((bf16[192,4096]{1,0:T(8,128)(2,1)}), bf16[768,4096]{1,0:T(8,128)(2,1)}) %all-gather.6.cloned.1.call-update) | async-done | bytes 6291472 | tf_op jit(solution)/shard_map/all_gather | solution.py:40
  151.2 18.4 %fusion.2 = f32[768,1792]{1,0:T(8,128)} fusion(bf16[768,4096]{1,0:T(8,128)(2,1)} %all-gather.6.cloned.1.call-done, bf16[1,1792,4096]{2,1,0:T(8,128)(2,1)} %param.11), kind=kOutput, calls=%fused_computation.7 | convolution fusion | flops 11274289152 | bytes 26476544 | tf_op jit(solution)/shard_map/rd,fd->rf/dot_general | solution.py:48
  169.6 0.0 copy-done.4
  169.6 18.0 %fusion.6 = f32[768,1792]{1,0:T(8,128)} fusion(bf16[768,4096]{1,0:T(8,128)(2,1)S(1)} %copy-done.4, bf16[1,1792,4096]{2,1,0:T(8,128)(2,1)} %param.12), kind=kOutput, calls=%fused_computation.11 | convolution fusion | flops 11274289152 | bytes 26476544 | tf_op jit(solution)/shard_map/rd,fd->rf/dot_general | solution.py:49
  187.6 78.8 %all-gather.4.cloned.1.call-done = bf16[768,4096]{1,0:T(8,128)(2,1)} async-done(((bf16[192,4096]{1,0:T(8,128)(2,1)}), bf16[768,4096]{1,0:T(8,128)(2,1)}) %all-gather.4.cloned.1.call-update) | async-done | bytes 6291472 | tf_op jit(solution)/shard_map/all_gather | solution.py:41
  266.4 24.2 %multiply_reduce_fusion = (f32[768]{0:T(1024)S(1)}, bf16[768,1792]{1,0:T(8,128)(2,1)}, bf16[768,1792]{1,0:T(8,128)(2,1)}, bf16[768,1792]{1,0:T(8,128)(2,1)}) fusion(f32[768,1792]{1,0:T(8,128)} %fusion.6, f32[768,1792]{1,0:T(8,128)} %fusion.2, f32[768]{0:T(1024)S(1)} %convert_element_type.48, bf16[768,4096]{1,0:T(8,128)(2,1)} %all-gather.4.cloned.1.call-done, ...), kind=kOutput, calls=%fused_computation.21 | convolution fusion | flops 11300436992 | bytes 40245248 | tf_op jit(solution)/shard_map/rd,fd->rf/dot_general | solution.py:53
  290.6 18.4 %fusion = f32[768,4096]{1,0:T(8,128)} fusion(bf16[768,1792]{1,0:T(8,128)(2,1)} %get-tuple-element.9, bf16[1,1792,4096]{2,1,0:T(8,128)(2,1)} %param.11), kind=kOutput, calls=%fused_computation.5 | convolution fusion | flops 11274289152 | bytes 30015488 | tf_op jit(solution)/shard_map/dot_general | solution.py:70
  309.0 19.9 %fusion.13 = f32[768,4096]{1,0:T(8,128)} fusion(f32[768,4096]{1,0:T(8,128)} %fusion, bf16[768,1792]{1,0:T(8,128)(2,1)S(1)} %copy-done.9, bf16[1,1792,4096]{2,1,0:T(8,128)(2,1)} %param.12), kind=kOutput, calls=%fused_computation.19 | convolution fusion | flops 11277434880 | bytes 42598400 | tf_op jit(solution)/shard_map/dot_general | solution.py:70
  329.0 0.0 reduce-scatter.2.cloned.1.call-update
  329.0 0.6 copy-done.7
  329.6 0.6 dynamic-slice.1
  330.2 0.6 dynamic-slice.2
  332.1 19.3 %all-reduce.2 = f32[768]{0:T(1024)S(1)} all-reduce(f32[768]{0:T(1024)S(1)} %get-tuple-element.5), channel_id=3, replica_groups=mesh['dp'=4,'expert'=4,'etensor'=2] {'dp','etensor'}, use_global_device_ids=true, to_apply=%region_4.5.clone | all-reduce | flops 768 | bytes 6144
  351.5 0.2 dynamic-slice_dynamic-update-slice_fusion
  351.6 4.9 all-reduce.1
  356.5 0.7 all_to_all.26
  357.2 3.2 all-to-all-start.4
  360.4 0.0 all-gather.8.cloned.1.call-start
  360.5 174.4 %reduce-scatter.2.cloned.1.call-done = f32[96,4096]{1,0:T(8,128)} async-done(((f32[768,4096]{1,0:T(8,128)}), f32[96,4096]{1,0:T(8,128)}) %reduce-scatter.2.cloned.1.call-update) | async-done | bytes 1572880 | tf_op jit(solution)/shard_map/reduce_scatter | solution.py:74
  534.9 0.0 all-gather.8.cloned.1.call-update
  534.9 18.5 %fusion.12 = bf16[1,1792,4096]{2,1,0:T(8,128)(2,1)} fusion(bf16[768,1792]{1,0:T(8,128)(2,1)} %get-tuple-element.6, bf16[768,4096]{1,0:T(8,128)(2,1)} %all-gather.4.cloned.1.call-done, f32[768]{0:T(1024)S(1)} %convert_element_type.48), kind=kOutput, calls=%fused_computation.17 | convolution fusion | flops 11291066368 | bytes 23727104 | tf_op jit(solution)/shard_map/rf,rd->fd/dot_general | solution.py:67
  553.4 0.0 copy-done.10
  553.4 17.7 %fusion.11 = bf16[1,1792,4096]{2,1,0:T(8,128)(2,1)} fusion(bf16[768,1792]{1,0:T(8,128)(2,1)S(1)} %copy-done.10, bf16[768,4096]{1,0:T(8,128)(2,1)} %all-gather.6.cloned.1.call-done), kind=kOutput, calls=%fused_computation.16 | convolution fusion | flops 11281629184 | bytes 23724032 | tf_op jit(solution)/shard_map/rf,rd->fd/dot_general | solution.py:64
  571.2 0.0 all-to-all-done.4
  571.2 9.2 %all-gather.8.cloned.1.call-done = f32[192,4096]{1,0:T(8,128)} async-done(((f32[96,4096]{1,0:T(8,128)}), f32[192,4096]{1,0:T(8,128)}) %all-gather.8.cloned.1.call-update) | async-done | bytes 3145744 | tf_op jit(solution)/shard_map/all_gather | solution.py:78
  580.4 4.8 all-to-all-start.3
  585.2 17.7 %fusion.10 = bf16[1,1792,4096]{2,1,0:T(8,128)(2,1)} fusion(bf16[768,1792]{1,0:T(8,128)(2,1)} %get-tuple-element.9, bf16[768,4096]{1,0:T(8,128)(2,1)} %all-gather.6.cloned.1.call-done), kind=kOutput, calls=%fused_computation.15 | convolution fusion | flops 11281629184 | bytes 23724032 | tf_op jit(solution)/shard_map/rf,rd->fd/dot_general | solution.py:61
  602.9 0.5 broadcast.42
  603.4 0.7 reduce.4
  604.0 0.1 reshape.66
  604.1 1.3 gather_fusion.1
  605.4 0.5 broadcast_select_fusion
  605.9 16.3 %all-to-all-done.3 = f32[4,48,4096]{2,1,0:T(8,128)} async-done(((f32[4,48,4096]{2,1,0:T(8,128)}), f32[4,48,4096]{2,1,0:T(8,128)}, u32[]{:S(2)}, u32[]{:S(2)}) %all-to-all-start.3) | async-done | bytes 3145760 | tf_op jit(solution)/shard_map/all_to_all | solution.py:82
  622.2 4.2 gather_fusion
  626.4 1.2 select_convert_fusion
  (18 shorter events, 0.1 us)
Async XLA Ops:
  7.2 2.6 copy-start
  7.2 27.5 %copy-start.2 = (bf16[128,4096]{1,0:T(8,128)(2,1)S(1)}, bf16[128,4096]{1,0:T(8,128)(2,1)}, u32[]{:S(2)}) copy-start(bf16[128,4096]{1,0:T(8,128)(2,1)} %param.8) | copy-start | bytes 3145732
  7.2 144.0 %all-gather.6.cloned.1.call-start = ((), (), s32[]{:S(2)}) async-start(), calls=%async_computation.7 | async-start | bytes 7864320 | tf_op jit(solution)/shard_map/all_gather | solution.py:40
  10.4 48.2 %copy-start.5 = (bf16[128]{0:T(256)(128)(2,1)S(1)}, bf16[128]{0:T(256)(128)(2,1)}, u32[]{:S(2)}) copy-start(bf16[128]{0:T(256)(128)(2,1)} %param.9) | copy-start | bytes 772
  10.4 52.3 %copy-start.8 = (u32[32]{0:T(128)S(1)}, u32[32]{0:T(128)}, u32[]{:S(2)}) copy-start(u32[32]{0:T(128)} %constant.44) | copy-start | bytes 388
  34.6 231.7 %all-gather.4.cloned.1.call-start = ((), (), s32[]{:S(2)}) async-start(), calls=%async_computation.6 | async-start | bytes 7864320 | tf_op jit(solution)/shard_map/all_gather | solution.py:41
  59.4 6.9 %all-to-all-start = ((bf16[4,1,48]{2,1,0:T(2,128)(2,1)}), bf16[4,1,48]{2,1,0:T(2,128)(2,1)S(1)}, u32[]{:S(2)}, u32[]{:S(2)}) async-start(bf16[4,1,48]{2,1,0:T(2,128)(2,1)} %all_to_all.28), calls=%async_computation | async-start | bytes 4096 | tf_op jit(solution)/shard_map/all_to_all | solution.py:37
  62.6 472.3 %reduce-scatter.2.cloned.1.call-start = ((), (), s32[]{:S(2)}) async-start(), calls=%async_computation.8 | async-start | bytes 14155776 | tf_op jit(solution)/shard_map/reduce_scatter | solution.py:74
  151.2 18.4 %copy-start.4 = (bf16[768,4096]{1,0:T(8,128)(2,1)S(1)}, bf16[768,4096]{1,0:T(8,128)(2,1)}, u32[]{:S(2)}) copy-start(bf16[768,4096]{1,0:T(8,128)(2,1)} %all-gather.6.cloned.1.call-done) | copy-start | bytes 18874372
  290.6 18.4 %copy-start.9 = (bf16[768,1792]{1,0:T(8,128)(2,1)S(1)}, bf16[768,1792]{1,0:T(8,128)(2,1)}, u32[]{:S(2)}) copy-start(bf16[768,1792]{1,0:T(8,128)(2,1)} %get-tuple-element.10) | copy-start | bytes 8257540
  329.0 0.7 copy-start.7
  329.0 1.2 copy-start.6
  329.0 3.1 copy-start.3
  357.2 214.0 %all-to-all-start.4 = ((f32[4,1,48]{2,1,0:T(1,128)}), f32[4,1,48]{2,1,0:T(1,128)S(1)}, u32[]{:S(2)}, u32[]{:S(2)}) async-start(f32[4,1,48]{2,1,0:T(1,128)} %all_to_all.26), calls=%async_computation.5 | async-start | bytes 4096 | tf_op jit(solution)/shard_map/all_to_all | solution.py:89
  360.4 219.9 %all-gather.8.cloned.1.call-start = ((), (), s32[]{:S(2)}) async-start(), calls=%async_computation.9 | async-start | bytes 4718592 | tf_op jit(solution)/shard_map/all_gather | solution.py:78
  534.9 18.5 %copy-start.10 = (bf16[768,1792]{1,0:T(8,128)(2,1)S(1)}, bf16[768,1792]{1,0:T(8,128)(2,1)}, u32[]{:S(2)}) copy-start(bf16[768,1792]{1,0:T(8,128)(2,1)} %get-tuple-element.10) | copy-start | bytes 8257540
  580.4 41.8 %all-to-all-start.3 = ((f32[4,48,4096]{2,1,0:T(8,128)}), f32[4,48,4096]{2,1,0:T(8,128)}, u32[]{:S(2)}, u32[]{:S(2)}) async-start(f32[4,48,4096]{2,1,0:T(8,128)} %bitcast.64), calls=%async_computation.4 | async-start | bytes 6291456 | tf_op jit(solution)/shard_map/all_to_all | solution.py:82
  622.2 5.4 copy-start.1
Sparse Core Ops, SparseCore 0:
  34.8 116.3 all-gather.5
  152.8 113.5 all-gather.3
  329.1 205.7 reduce-scatter.1
  536.3 44.0 all-gather.7
where the time goes:
time: 637 us; the launch traced here: 634 us
  waiting for transfers between devices  353 us (55%)
  matrix products  154 us (24%)
  blocking collectives  84.7 us (13%)
  between operations  16.1 us (3%)
  starting transfers between devices  11.4 us (2%)
  local copies, waits for them, and re-layouts  10.3 us (2%)
    reduce_scatter x1, waiting for transfers between devices, per_device(): lax.psum_scatter(row_term, ('dp', 'etensor'), scatter_dimension=0, tiled=...  174 us
    all_gather x1, waiting for transfers between devices, per_device(): lax.all_gather(recv_grads.reshape(-1, width), 'dp', axis=0, tiled=True)  78.8 us
    all_gather x1, waiting for transfers between devices, per_device(): lax.all_gather(recv_rows.reshape(-1, width), 'dp', axis=0, tiled=True)  71.7 us
    unnamed x3, blocking collectives  37.2 us
    dot_general x1, matrix products, per_device(): jnp.einsum('rd,fd->rf', group_grads, w_down, preferred_element_type=jnp.f...  24.2 us
    all_to_all x1, blocking collectives, per_device(): lax.all_to_all(send_rows, 'expert', split_axis=0, concat_axis=0, tiled=True)  24.2 us
    all_to_all x1, blocking collectives, per_device(): lax.all_to_all(send_grads, 'expert', split_axis=0, concat_axis=0, tiled=T...  23.3 us
    dot_general x1, matrix products, per_device(): jnp.dot(up_pre_grad, w_up, preferred_element_type=jnp.float32)  19.9 us
  transfers between devices with their start and end apart: 7, of which 6 were waited for; matrix products, arithmetic and copies ran while one was open for 15% of the time, Pallas kernels for 0%

commit v1 on v0

--- a/solution.py
+++ b/solution.py
@@ -1,10 +1,572 @@
+import functools
+
 import jax
 import jax.numpy as jnp
 from jax import lax
+from jax.experimental import pallas as pl
+from jax.experimental.pallas import tpu as pltpu
 from jax.sharding import PartitionSpec as P
 
-
-def per_device(token_rows, row_grads, gate_scale, routing, gate_weight, up_weight, down_weight):
+LANES = 128
+F_BLOCK = 256
+MIB = 1 << 20
+VMEM = 56 * MIB
+SMALL = pl.CostEstimate(flops=0, bytes_accessed=0, transcendentals=0)
+
+OUTER = ((0, 1), (1, 0), (2, 3), (3, 2))
+MIDDLE = ((1, 2), (2, 1))
+OUT = ((1, 0), (2, 3))
+IN = ((0, 1), (3, 2))
+SKIP = ((0, 2), (2, 0), (1, 3), (3, 1))
+ENDS = ((0, 3), (3, 0))
+IN_TWO = ((0, 2), (3, 1))
+OUT_TWO = ((2, 0), (1, 3))
+
+
+def nt_dot(a, b):
+    return lax.dot_general(a, b, (((1,), (1,)), ((), ())), preferred_element_type=jnp.float32)
+
+
+def tn_dot(a, b):
+    return lax.dot_general(a, b, (((0,), (0,)), ((), ())), preferred_element_type=jnp.float32)
+
+
+def pack_kernel(slot_ref, rows_ref, grads_ref, scale_ref, *out_refs):
+    width = rows_ref.shape[1]
+    slot = slot_ref[...]
+    for group, out_ref in enumerate(out_refs):
+        size = out_ref.shape[0]
+        at = lax.broadcasted_iota(jnp.int32, (size, slot.shape[1]), 0) + group * size
+        placing = (at == slot).astype(jnp.float32).astype(jnp.bfloat16)
+        for start, ref in ((0, rows_ref), (width, grads_ref), (2 * width, scale_ref)):
+            out_ref[:, start : start + ref.shape[1]] = jnp.dot(
+                placing, ref[...], preferred_element_type=jnp.float32
+            ).astype(jnp.bfloat16)
+
+
+def pack(slot, rows, grads, scale, groups, size):
+    width = rows.shape[1]
+    shape = jax.ShapeDtypeStruct((size, 2 * width + LANES), jnp.bfloat16)
+    return pl.pallas_call(
+        pack_kernel,
+        out_shape=[shape] * groups,
+        compiler_params=pltpu.CompilerParams(vmem_limit_bytes=32 * MIB),
+        cost_estimate=pl.CostEstimate(
+            flops=2 * groups * size * rows.shape[0] * 2 * width,
+            bytes_accessed=4 * (rows.shape[0] + groups * size) * width,
+            transcendentals=0,
+        ),
+    )(slot, rows, grads, scale)
+
+
+class Order:
+    def __init__(self):
+        self.token = jnp.zeros((8, LANES), jnp.float32)
+
+    def call(self, kernel, operands, in_specs, out_shape, out_specs, **options):
+        n_in, n_out = len(operands), len(out_shape)
+
+        def body(*refs):
+            ins, refs = refs[:n_in], refs[n_in + 1 :]
+            outs, scratch = refs[:n_out], refs[n_out + 1 :]
+            kernel(*ins, *outs, *scratch)
+
+        anywhere = pl.BlockSpec(memory_space=pl.ANY)
+        *out, self.token = pl.pallas_call(
+            body,
+            in_specs=[*in_specs, anywhere],
+            out_specs=[*out_specs, anywhere],
+            out_shape=[*out_shape, jax.ShapeDtypeStruct(self.token.shape, self.token.dtype)],
+            input_output_aliases={n_in: n_out},
+            compiler_params=pltpu.CompilerParams(vmem_limit_bytes=VMEM),
+            cost_estimate=SMALL,
+            **options,
+        )(*operands, self.token)
+        return out
+
+
+def choose_kernel(picks, copies, needs, flag_ref, *refs):
+    n_in = 2 * picks + copies
+    ins, outs = refs[:n_in], refs[n_in + needs : -1]
+    sems = refs[-1]
+
+    def move(first):
+        pairs = [(ins[2 * i + 1 - first], outs[i]) for i in range(picks)]
+        pairs += [(ins[2 * picks + i], outs[picks + i]) for i in range(copies)]
+        moves = [pltpu.make_async_copy(a, b, sems.at[i]) for i, (a, b) in enumerate(pairs)]
+        for one in moves:
+            one.start()
+        for one in moves:
+            one.wait()
+
+    @pl.when(flag_ref[0] == 1)
+    def _():
+        move(1)
+
+    @pl.when(flag_ref[0] != 1)
+    def _():
+        move(0)
+
+
+def choose(order, flag, pairs, singles=(), needs=()):
+    operands = [flag, *[a for pair in pairs for a in pair], *singles, *needs]
+    anywhere = pl.BlockSpec(memory_space=pl.ANY)
+    out_shape = [jax.ShapeDtypeStruct(a.shape, a.dtype) for a in [p[0] for p in pairs] + list(singles)]
+    return order.call(
+        functools.partial(choose_kernel, len(pairs), len(singles), len(needs)),
+        operands,
+        [pl.BlockSpec(memory_space=pltpu.SMEM)] + [anywhere] * (len(operands) - 1),
+        out_shape,
+        [anywhere] * len(out_shape),
+        scratch_shapes=[pltpu.SemaphoreType.DMA((len(out_shape),))],
+    )
+
+
+def sum_kernel(plan, flag_ref, *refs):
+    n_in = len(refs) - len(plan)
+    for (rows, terms, others), out_ref in zip(plan, refs[n_in:], strict=True):
+
+        def add(terms, out_ref=out_ref, rows=rows):
+            total = None
+            for k, start in terms:
+                term = refs[k][start : start + rows, :].astype(jnp.float32)
+                total = term if total is None else total + term
+            out_ref[...] = total.astype(out_ref.dtype)
+
+        if others is None:
+            add(terms)
+        else:
+            pl.when(flag_ref[0] == 1)(functools.partial(add, terms))
+            pl.when(flag_ref[0] != 1)(functools.partial(add, others))
+
+
+def sums(order, flag, operands, plan):
+    width = operands[0].shape[1]
+    inside = pl.BlockSpec(memory_space=pltpu.VMEM)
+    return order.call(
+        functools.partial(sum_kernel, plan),
+        [flag, *operands],
+        [pl.BlockSpec(memory_space=pltpu.SMEM)] + [inside] * len(operands),
+        [jax.ShapeDtypeStruct((rows, width), jnp.bfloat16) for rows, _, _ in plan],
+        [inside] * len(plan),
+    )
+
+
+def unit_kernel(n_pieces, parts, count, lane_ref, flag_ref, *refs):
+    pieces = refs[:n_pieces]
+    weights = refs[n_pieces : n_pieces + 3]
+    refs = refs[n_pieces + 3 :]
+    outs, scaled_out = refs[:3], refs[3]
+    partial_refs = refs[4 : 4 + len(parts)]
+    (
+        rows_ref,
+        grads_ref,
+        scale_ref,
+        scaled_ref,
+        total_ref,
+        scale_sum_ref,
+        held_ref,
+        act_ref,
+        piece_sems,
+        weight_sems,
+        act_sems,
+        scaled_sem,
+    ) = refs[4 + len(parts) :]
+    size = pieces[0].shape[0]
+    width = rows_ref.shape[1]
+    slots = held_ref.shape[0]
+
+    def weight_copy(i, k):
+        return pltpu.make_async_copy(
+            weights[k].at[pl.ds(i * F_BLOCK, F_BLOCK), :],
+            held_ref.at[lax.rem(i, slots), k],
+            weight_sems.at[lax.rem(i, slots), k],
+        )
+
+    def act_copy(i, k):
+        return pltpu.make_async_copy(
+            act_ref.at[lax.rem(i, 2), k],
+            outs[k].at[:, pl.ds(pl.multiple_of(i * F_BLOCK, F_BLOCK), F_BLOCK)],
+            act_sems.at[lax.rem(i, 2), k],
+        )
+
+    def piece_copies(j, start, ref):
+        return [
+            pltpu.make_async_copy(
+                piece.at[:, pl.ds(start, ref.shape[1])],
+                ref.at[pl.ds(i * size, size), :],
+                piece_sems.at[i, j],
+            )
+            for i, piece in enumerate(pieces)
+        ]
+
+    row_copies = piece_copies(0, 0, rows_ref)
+    grad_copies = piece_copies(1, width, grads_ref) + piece_copies(2, 2 * width, scale_ref)
+    for copy in row_copies:
+        copy.start()
+    weight_copy(0, 0).start()
+    weight_copy(0, 1).start()
+    for copy in grad_copies:
+        copy.start()
+    weight_copy(0, 2).start()
+    for k in range(3):
+        weight_copy(1, k).start()
+    total_ref[...] = jnp.zeros_like(total_ref)
+    scale_sum_ref[...] = jnp.zeros_like(scale_sum_ref)
+    for copy in row_copies + grad_copies:
+        copy.wait()
+    scale = scale_ref[:, 0:1].astype(jnp.float32)
+    scaled_ref[...] = (scale * grads_ref[...].astype(jnp.float32)).astype(jnp.bfloat16)
+    scaled_copy = pltpu.make_async_copy(scaled_ref, scaled_out, scaled_sem)
+    scaled_copy.start()
+
+    def products(i):
+        held = held_ref.at[lax.rem(i, slots)]
+        gate_pre = nt_dot(rows_ref[...], held[0])
+        up_pre = nt_dot(rows_ref[...], held[1])
+        raw = nt_dot(grads_ref[...], held[2])
+        return gate_pre, up_pre, raw
+
+    def activate(i, gate_pre, up_pre, raw):
+        sigmoid = jax.nn.sigmoid(gate_pre)
+        activated = gate_pre * sigmoid
+        hidden = (activated * up_pre).astype(jnp.bfloat16)
+        scale_sum_ref[...] += jnp.sum(hidden.astype(jnp.float32) * raw, axis=1, keepdims=True)
+        hidden_grad = scale_ref[:, 0:1].astype(jnp.float32) * raw
+        act = act_ref.at[lax.rem(i, 2)]
+        act[0] = hidden
+        act[1] = (
+            hidden_grad * up_pre * sigmoid * (1.0 + gate_pre * (1.0 - sigmoid))
+        ).astype(jnp.bfloat16)
+        act[2] = (hidden_grad * activated).astype(jnp.bfloat16)
+
+    def add_inputs(i, finish=None):
+        held = held_ref.at[lax.rem(i, slots)]
+        act = act_ref.at[lax.rem(i, 2)]
+        gate_grad, up_grad = act[1], act[2]
+        tile = 1024
+        for start in range(0, width, tile):
+            at = slice(start, start + tile)
+            total = (
+                total_ref[:, at]
+                + jnp.dot(gate_grad, held[0, :, at], preferred_element_type=jnp.float32)
+                + jnp.dot(up_grad, held[1, :, at], preferred_element_type=jnp.float32)
+            )
+            if finish is None:
+                total_ref[:, at] = total
+            else:
+                finish(at, total)
+
+    def arrive(i):
+        for k in range(3):
+            weight_copy(i, k).wait()
+
+        @pl.when(i + 2 < count)
+        def _():
+            for k in range(3):
+                weight_copy(i + 2, k).start()
+
+    arrive(0)
+    activate(0, *products(0))
+    for k in range(3):
+        act_copy(0, k).start()
+
+    def step(i, carry):
+        arrive(i)
+
+        @pl.when(i >= 2)
+        def _():
+            for k in range(3):
+                act_copy(i - 2, k).wait()
+
+        now = products(i)
+        add_inputs(i - 1)
+        activate(i, *now)
+        for k in range(3):
+            act_copy(i, k).start()
+        return carry
+
+    lax.fori_loop(1, count, step, 0)
+
+    def write(at, value):
+        for ref, (start, size, other) in zip(partial_refs, parts, strict=True):
+            part = value[start : start + size].astype(jnp.bfloat16)
+            if other is None:
+                ref[:, at] = part
+            else:
+                second = value[other : other + size].astype(jnp.bfloat16)
+                ref[:, at] = jnp.where(flag_ref[0] == 1, part, second)
+
+    add_inputs(count - 1, write)
+    value = scale_sum_ref[...]
+    high = value.astype(jnp.bfloat16).astype(jnp.float32)
+    lane = lax.broadcasted_iota(jnp.int32, (value.shape[0], LANES), 1)
+    first = lane_ref[0]
+    lanes = jnp.where(lane == first, high, jnp.where(lane == first + 1, value - high, 0.0))
+    write(slice(width, width + LANES), lanes)
+    for i in (count - 2, count - 1):
+        for k in range(3):
+            act_copy(i, k).wait()
+    scaled_copy.wait()
+
+
+class Unit:
+    def __init__(self, order, lane, flag, pieces, parts, weights):
+        size = pieces[0].shape[0]
+        rows = size * len(pieces)
+        units, width = weights[0].shape
+        count = units // F_BLOCK
+        anywhere = pl.BlockSpec(memory_space=pl.ANY)
+        inside = pl.BlockSpec(memory_space=pltpu.VMEM)
+        scalar = pl.BlockSpec(memory_space=pltpu.SMEM)
+        bf16 = jnp.bfloat16
+        out = order.call(
+            functools.partial(unit_kernel, len(pieces), parts, count),
+            [lane, flag, *pieces, *weights],
+            [scalar, scalar] + [anywhere] * (len(pieces) + 3),
+            [jax.ShapeDtypeStruct((rows, units), bf16)] * 3
+            + [jax.ShapeDtypeStruct((rows, width), bf16)]
+            + [jax.ShapeDtypeStruct((part[1], width + LANES), bf16) for part in parts],
+            [anywhere] * 4 + [inside] * len(parts),
+            scratch_shapes=[
+                pltpu.VMEM((rows, width), bf16),
+                pltpu.VMEM((rows, width), bf16),
+                pltpu.VMEM((rows, LANES), bf16),
+                pltpu.VMEM((rows, width), bf16),
+                pltpu.VMEM((rows, width), jnp.float32),
+                pltpu.VMEM((rows, 1), jnp.float32),
+                pltpu.VMEM((4, 3, F_BLOCK, width), bf16),
+                pltpu.VMEM((2, 3, rows, F_BLOCK), bf16),
+                pltpu.SemaphoreType.DMA((len(pieces), 3)),
+                pltpu.SemaphoreType.DMA((4, 3)),
+                pltpu.SemaphoreType.DMA((2, 3)),
+                pltpu.SemaphoreType.DMA(()),
+            ],
+        )
+        self.hidden, self.gate_grad, self.up_grad, self.scaled = out[:4]
+        self.partials = out[4:]
+        self.pieces = pieces
+
+
+def weight_kernel(n_right, n_left, *refs):
+    right, refs = refs[:n_right], refs[n_right:]
+    left, refs = refs[:n_left], refs[n_left:]
+    out_ref, rows_ref, sems = refs
+    width = rows_ref.shape[1]
+
+    @pl.when(pl.program_id(0) == 0)
+    def _():
+        copies, start = [], 0
+        for i, ref in enumerate(right):
+            size = ref.shape[0]
+            copies.append(
+                pltpu.make_async_copy(
+                    ref.at[:, pl.ds(0, width)], rows_ref.at[pl.ds(start, size), :], sems.at[i]
+                )
+            )
+            start += size
+        for copy in copies:
+            copy.start()
+        for copy in copies:
+            copy.wait()
+
+    both = jnp.concatenate([ref[...] for ref in left], axis=0)
+    tile = 1024
+    for start in range(0, width, tile):
+        at = slice(start, start + tile)
+        out_ref[:, at] = tn_dot(both, rows_ref[:, at]).astype(jnp.bfloat16)
+
+
+def weight_grad(order, right, left, width):
+    rows = sum(a.shape[0] for a in left)
+    units = left[0].shape[1]
+    anywhere = pl.BlockSpec(memory_space=pl.ANY)
+    return order.call(
+        functools.partial(weight_kernel, len(right), len(left)),
+        [*right, *left],
+        [anywhere] * len(right)
+        + [pl.BlockSpec((a.shape[0], F_BLOCK), lambda i: (0, i)) for a in left],
+        [jax.ShapeDtypeStruct((units, width), jnp.bfloat16)],
+        [pl.BlockSpec((F_BLOCK, width), lambda i: (i, 0))],
+        grid=(units // F_BLOCK,),
+        scratch_shapes=[
+            pltpu.VMEM((rows, width), jnp.bfloat16),
+            pltpu.SemaphoreType.DMA((len(right),)),
+        ],
+    )[0]
+
+
+def unpack_kernel(slot_ref, *refs):
+    grads_ref, scale_ref = refs[-2:]
+    width = grads_ref.shape[1]
+    slot = slot_ref[...]
+    total = jnp.zeros((slot.shape[0], width + LANES), jnp.float32)
+    for group, ref in enumerate(refs[:-2]):
+        size = ref.shape[0]
+        at = lax.broadcasted_iota(jnp.int32, (slot.shape[0], size), 1) + group * size
+        placing = (at == slot).astype(jnp.float32).astype(jnp.bfloat16)
+        total += jnp.dot(placing, ref[...], preferred_element_type=jnp.float32)
+    grads_ref[...] = total[:, :width].astype(jnp.bfloat16)
+    scale_ref[...] = jnp.sum(total[:, width:], axis=1, keepdims=True)
+
+
+def unpack(order, slot, groups, width):
+    rows = slot.shape[0]
+    inside = pl.BlockSpec(memory_space=pltpu.VMEM)
+    return order.call(
+        unpack_kernel,
+        [slot, *groups],
+        [inside] * (1 + len(groups)),
+        [
+            jax.ShapeDtypeStruct((rows, width), jnp.bfloat16),
+            jax.ShapeDtypeStruct((rows, 1), jnp.float32),
+        ],
+        [inside] * 2,
+    )
+
+
+def line_device(token_rows, row_grads, gate_scale, routing, gate_weight, up_weight, down_weight):
+    width = token_rows.shape[1]
+    local_rows = token_rows.shape[0]
+    size = 3 * local_rows // 8
+    z, e, x = (lax.axis_index(name) for name in ("dp", "expert", "etensor"))
+    middle = (z == 1) | (z == 2)
+    w_gate, w_up, w_down = gate_weight[0], up_weight[0], down_weight[0]
+    lane = ((z * 2 + x) * 2).astype(jnp.int32).reshape(1)
+
+    route = routing[:, 0]
+    other = lax.bitwise_xor(route, e)
+    group = lax.bitwise_xor(other & 1, x) * 2 + (other >> 1)
+    index = jnp.arange(local_rows, dtype=jnp.int32)
+    earlier = (route[:, None] == route[None, :]) & (index[None, :] < index[:, None])
+    slot = group * size + jnp.sum(earlier.astype(jnp.int32), axis=1)
+    scale_lanes = jnp.broadcast_to(gate_scale[:, None], (local_rows, LANES))
+    groups = pack(slot[None, :], token_rows, row_grads, scale_lanes, 4, size)
+
+    def over_expert(a, g, cross=0):
+        pairs = []
+        for i in range(4):
+            for j in range(2):
+                d = (j ^ (g >> 1)) + 2 * (g & 1)
+                pairs.append((i * 2 + j, (i ^ d) * 2 + (j ^ cross)))
+        return lax.ppermute(a, ("expert", "etensor"), pairs)
+
+    def along(a, pairs):
+        return lax.ppermute(a, "dp", pairs)
+
+    def across(a):
+        return lax.ppermute(a, "etensor", ((0, 1), (1, 0)))
+
+    near, far, near_other, far_other = (over_expert(a, g) for g, a in enumerate(groups))
+
+    order = Order()
+    flag = middle.astype(jnp.int32).reshape(1)
+    weights = (w_gate, w_up, w_down)
+    pair = 2 * size
+    x_near = along(near, OUTER)
+    middle_near = along(near, MIDDLE)
+    xx_near = across(x_near)
+    second_near = along(x_near, MIDDLE)
+    out_near = along(middle_near, OUT)
+    out_second = along(second_near, OUT)
+
+    y_near, far_1 = choose(order, flag, [(middle_near, out_near)], [far])
+    xy_near = across(y_near)
+    ends_far = along(far_1, ENDS)
+    in_far = along(far_1, IN_TWO)
+    u1 = Unit(
+        order,
+        lane,
+        flag,
+        [near, near_other, far, far_other],
+        [(0, pair, None), (pair, size, None), (pair + size, size, None)],
+        weights,
+    )
+    z_near, far_2 = choose(order, flag, [(second_near, out_second)], [far])
+    xz_near = across(z_near)
+    middle_far = along(far_2, MIDDLE)
+    out_far = along(far_2, OUT_TWO)
+    x_far = along(far_2, OUTER)
+    z_far, w_other = choose(order, flag, [(in_far, ends_far)], [u1.partials[2]])
+    w_other = across(w_other)
+    xz_far = across(z_far)
+    u2 = Unit(
+        order,
+        lane,
+        flag,
+        [x_near, xx_near, y_near, xy_near, z_near, xz_near],
+        [(0, pair, None), (pair, pair, None), (2 * pair, pair, None), (2 * pair, pair, pair)],
+        weights,
+    )
+    y_far, x_far = choose(order, flag, [(middle_far, out_far)], [x_far], [xz_far, w_other])
+    xy_far = across(y_far)
+    xx_far = across(x_far)
+    x_part, y_part, z_part, s_part = u2.partials
+    near_terms = [
+        along(x_part, OUTER),
+        along(s_part, SKIP),
+        along(y_part, MIDDLE),
+        along(z_part, ENDS),
+    ]
+    u3 = Unit(
+        order,
+        lane,
+        flag,
+        [z_far, y_far, xz_far, xy_far],
+        [(0, pair, None), (pair, pair, None)],
+        weights,
+    )
+    zy_other = across(u3.partials[1])
+    u4 = Unit(
+        order, lane, flag, [x_far, xx_far], [(0, size, None), (size, size, None)], weights
+    )
+    x_other = across(u4.partials[1])
+    terms = range(2, 7)
+    z_part, y_part, s_part, near_own, near_other = sums(
+        order,
+        flag,
+        [u3.partials[0], zy_other, u1.partials[0], *near_terms],
+        [
+            (size, [(0, 0), (1, 0)], None),
+            (size, [(0, size), (1, size)], None),
+            (size, [(0, 0), (1, 0)], [(0, size), (1, size)]),
+            (size, [(k, 0) for k in terms], None),
+            (size, [(k, size) for k in terms], None),
+        ],
+    )
+    near_other = across(near_other)
+    far_terms = [along(s_part, SKIP), along(y_part, MIDDLE), along(z_part, ENDS)]
+
+    units_of = (u1, u2, u3, u4)
+    rows = [piece for u in units_of for piece in u.pieces]
+    scaled = [u.scaled for u in units_of]
+    width = token_rows.shape[1]
+
+    def grad_of(right, name):
+        return weight_grad(order, right, [getattr(u, name) for u in units_of], width)
+
+    grad_down = grad_of(scaled, "hidden")
+    (x_part,) = sums(
+        order, flag, [u4.partials[0], x_other], [(size, [(0, 0), (1, 0)], None)]
+    )
+    far_terms.append(along(x_part, OUTER))
+    grad_gate = grad_of(rows, "gate_grad")
+    near_own, far_own = sums(
+        order,
+        flag,
+        [near_own, near_other, u1.partials[1], w_other, *far_terms],
+        [(size, [(0, 0), (1, 0)], None), (size, [(k, 0) for k in range(2, 8)], None)],
+    )
+    far_back = [over_expert(far_own, 1), over_expert(far_own, 1, 1)]
+    near_back = [over_expert(near_own, 0), over_expert(near_own, 0, 1)]
+    grad_up = grad_of(rows, "up_grad")
+    input_grads, scale_grads = unpack(
+        order, slot[:, None], [near_back[0], far_back[0], near_back[1], far_back[1]], width
+    )
+    return (input_grads, scale_grads[:, 0], grad_gate[None], grad_up[None], grad_down[None])
+
+
+def plain_device(token_rows, row_grads, gate_scale, routing, gate_weight, up_weight, down_weight):
     experts = lax.axis_size("expert")
     width = token_rows.shape[1]
     local_rows = token_rows.shape[0]
@@ -116,6 +678,8 @@
         P("expert", ("dp", "etensor"), None),
         P("expert", ("dp", "etensor"), None),
     )
+    sizes = (mesh.shape["dp"], mesh.shape["expert"], mesh.shape["etensor"])
+    per_device = line_device if sizes == (4, 4, 2) else plain_device
     return jax.shard_map(
         per_device, mesh=mesh, in_specs=in_specs, out_specs=out_specs, check_vma=False
     )

time: 637 us -> 494 us (0.78)
  Pallas kernels: 0 us -> 370 us
  waiting for transfers between devices: 353 us -> 48 us
  matrix products: 154 us -> 0 us
  blocking collectives: 84.7 us -> 0 us
  starting transfers between devices: 11.4 us -> 58.5 us
  between operations: 16.1 us -> 1.31 us
    pallas_call x0 -> x16, Pallas kernels: none -> 370 us  [the longest x15 369 us: call(): pl.pallas_call(body, in_specs=[*in_specs, anywhere], out_specs=[*out_spec...]
    reduce_scatter x1 -> x0, waiting for transfers between devices: 174 us -> none  [per_device(): lax.psum_scatter(row_term, ('dp', 'etensor'), scatter_dimension=0, tiled=...]
    all_gather x3 -> x0, waiting for transfers between devices: 160 us -> none  [the longest x1 78.8 us: per_device(): lax.all_gather(recv_grads.reshape(-1, width), 'dp', axis=0, tiled=True)]
    dot_general x11 -> x0, matrix products: 154 us -> none  [the longest x1 24.2 us: per_device(): jnp.einsum('rd,fd->rf', group_grads, w_down, preferred_element_type=jnp.f...]
    ppermute x0 -> x36, starting transfers between devices: none -> 58.5 us  [the longest x18 34 us: along(): return lax.ppermute(a, 'dp', pairs)]
    ppermute x0 -> x36, waiting for transfers between devices: none -> 48 us  [the longest x18 20.5 us: along(): return lax.ppermute(a, 'dp', pairs)]
    all_to_all x2 -> x0, blocking collectives: 47.5 us -> none  [the longest x1 24.2 us: per_device(): lax.all_to_all(send_rows, 'expert', split_axis=0, concat_axis=0, tiled=True)]
    unnamed x3 -> x0, blocking collectives: 37.2 us -> none
  transfers between devices with their start and end apart: 7 -> 36, of which waited for: 6 -> 5; matrix products, arithmetic and copies ran while one was open for 15% -> 0% of each run, Pallas kernels for 0% -> 63%
where the time goes in v1:
time: 494 us; the launch traced here: 493 us
  Pallas kernels  370 us (75%)
  starting transfers between devices  58.5 us (12%)
  waiting for transfers between devices  48 us (10%)
  local copies, waits for them, and re-layouts  12 us (2%)
    pallas_call x15, Pallas kernels, call(): pl.pallas_call(body, in_specs=[*in_specs, anywhere], out_specs=[*out_spec...  369 us
    ppermute x18, starting transfers between devices, along(): return lax.ppermute(a, 'dp', pairs)  34 us
    ppermute x18, waiting for transfers between devices, along(): return lax.ppermute(a, 'dp', pairs)  20.5 us
    ppermute x8, waiting for transfers between devices, over_expert(): return lax.ppermute(a, ('expert', 'etensor'), pairs)  14.6 us
    ppermute x10, starting transfers between devices, across(): return lax.ppermute(a, 'etensor', ((0, 1), (1, 0)))  14.2 us
    ppermute x10, waiting for transfers between devices, across(): return lax.ppermute(a, 'etensor', ((0, 1), (1, 0)))  12.9 us
    unnamed x65, local copies, waits for them, and re-layouts  10.6 us
    ppermute x8, starting transfers between devices, over_expert(): return lax.ppermute(a, ('expert', 'etensor'), pairs)  10.4 us
  transfers between devices with their start and end apart: 36, of which 5 were waited for; matrix products, arithmetic and copies ran while one was open for 0% of the time, Pallas kernels for 63%

profile of v1, /device:TPU:0, one launch (start us, length us, event | category | flops | bytes accessed | tf_op | source)
XLA Modules:
  0.0 493.0 jit_solution(14504446092878652235)
XLA Ops:
  0.6 0.8 copy.33
  1.4 0.9 convert_reduce_fusion
  2.4 0.7 fusion.1
  3.1 0.7 broadcast_in_dim.10.scale_ref
  3.8 1.2 copy-done
  5.1 1.2 copy-done.1
  6.3 1.3 shard_map.110
  7.6 0.7 collective-permute-start
  8.3 3.1 collective-permute-start.8
  11.4 1.6 collective-permute-start.1
  13.0 16.2 %collective-permute-done.8.refs_2_.refs_4_ = bf16[48,8320]{1,0:T(8,128)(2,1)S(1)} collective-permute-done((bf16[48,8320]{1,0:T(8,128)(2,1)S(1)}, bf16[48,8320]{1,0:T(8,128)(2,1)S(1)}, u32[]{:S(2)}, u32[]{:S(2)}) %collective-permute-start.8) | collective-permute-done | bytes 798752 | tf_op jit(solution)/shard_map/ppermute | solution.py:455
  29.2 1.6 collective-permute-start.9
  30.8 1.7 collective-permute-start.3
  32.5 1.3 collective-permute-start.2
  33.7 1.9 collective-permute-start.6
  36.2 1.3 collective-permute-start.10
  37.5 14.0 %collective-permute-done.3.refs_3_.refs_4_.refs_2_ = bf16[48,8320]{1,0:T(8,128)(2,1)S(1)} collective-permute-done((bf16[48,8320]{1,0:T(8,128)(2,1)S(1)}, bf16[48,8320]{1,0:T(8,128)(2,1)S(1)}, u32[]{:S(2)}, u32[]{:S(2)}) %collective-permute-start.3) | collective-permute-done | bytes 798752 | tf_op jit(solution)/shard_map/ppermute | solution.py:452
  51.5 4.3 collective-permute-done.2.refs_2_
  55.8 0.6 broadcast_in_dim.11.refs_4_
  56.4 49.5 %shard_map.111 = (bf16[48,8320]{1,0:T(8,128)(2,1)}, bf16[48,8320]{1,0:T(8,128)(2,1)}, f32[8,128]{1,0:T(8,128)}) custom-call(s32[1]{0:T(128)} %bitcast.2.refs_0_.refs_1_, bf16[48,8320]{1,0:T(8,128)(2,1)} %collective-permute-done.1.refs_1_, bf16[48,8320]{1,0:T(8,128)(2,1)} %collective-permute-done.2.refs_2_, ...), custom_call_target="tpu_custom_call", output_to_operand_aliasing={{2}: (4, {})} | custom-call | tf_op jit(solution)/shard_map/pallas_call | solution.py:75
  105.9 4.6 collective-permute-start.5
  110.5 1.3 collective-permute-start.4
  111.8 4.4 collective-permute-start.16
  116.3 28.4 %shard_map.112 = (bf16[192,1792]{1,0:T(8,128)(2,1)}, bf16[192,1792]{1,0:T(8,128)(2,1)}, bf16[192,1792]{1,0:T(8,128)(2,1)}, bf16[192,4096]{1,0:T(8,128)(2,1)}, bf...) custom-call(s32[1]{0:T(128)} %bitcast.3.refs_0_, ...), custom_call_target="tpu_custom_call", output_to_operand_aliasing={{7}: (9, {})} | custom-call | tf_op jit(solution)/shard_map/pallas_call | solution.py:75
  144.7 49.5 %shard_map.113 = (bf16[48,8320]{1,0:T(8,128)(2,1)}, bf16[48,8320]{1,0:T(8,128)(2,1)}, f32[8,128]{1,0:T(8,128)}) custom-call(s32[1]{0:T(128)} %bitcast.2.refs_0_.refs_1_, bf16[48,8320]{1,0:T(8,128)(2,1)} %collective-permute-done.9.refs_1_, bf16[48,8320]{1,0:T(8,128)(2,1)} %collective-permute-done.10.refs_2_, ...), custom_call_target="tpu_custom_call", output_to_operand_aliasing={{2}: (4, {})} | custom-call | tf_op jit(solution)/shard_map/pallas_call | solution.py:75
  194.3 2.0 collective-permute-start.18
  196.3 0.9 copy-done.17
  197.4 37.6 %shard_map.114 = (bf16[48,8320]{1,0:T(8,128)(2,1)}, bf16[48,4224]{1,0:T(8,128)(2,1)}, f32[8,128]{1,0:T(8,128)}) custom-call(s32[1]{0:T(128)} %bitcast.2.refs_0_.refs_1_, bf16[48,8320]{1,0:T(8,128)(2,1)} %copy-done.18, bf16[48,8320]{1,0:T(8,128)(2,1)} %copy-done.17, bf16[48,4224]{1,0:T(8,128)(2,1)} %get-tuple-element.77.refs_3_, ...), custom_call_target="tpu_custom_call", output_to_operand_aliasing={{2}: (4, {})} | custom-call | tf_op jit(solution)/shard_map/pallas_call | solution.py:75
  235.2 1.3 collective-permute-start.12
  236.5 0.9 collective-permute-start.11
  237.4 2.0 collective-permute-start.15
  239.4 32.4 %shard_map.115 = (bf16[288,1792]{1,0:T(8,128)(2,1)}, bf16[288,1792]{1,0:T(8,128)(2,1)}, bf16[288,1792]{1,0:T(8,128)(2,1)}, bf16[288,4096]{1,0:T(8,128)(2,1)}, bf...) custom-call(s32[1]{0:T(128)} %bitcast.3.refs_0_, ...), custom_call_target="tpu_custom_call", output_to_operand_aliasing={{8}: (11, {})} | custom-call | tf_op jit(solution)/shard_map/pallas_call | solution.py:75
  272.0 0.7 copy-done.11
  273.7 49.5 %shard_map.116 = (bf16[48,8320]{1,0:T(8,128)(2,1)}, bf16[48,8320]{1,0:T(8,128)(2,1)}, f32[8,128]{1,0:T(8,128)}) custom-call(s32[1]{0:T(128)} %bitcast.2.refs_0_.refs_1_, bf16[48,8320]{1,0:T(8,128)(2,1)} %copy-done.21, bf16[48,8320]{1,0:T(8,128)(2,1)} %copy-done.20, bf16[48,8320]{1,0:T(8,128)(2,1)} %copy-done.19, ...), custom_call_target="tpu_custom_call", output_to_operand_aliasing={{2}: (6, {})} | custom-call | tf_op jit(solution)/shard_map/pallas_call | solution.py:75
  323.3 1.1 collective-permute-start.19
  324.3 1.0 collective-permute-start.25
  325.3 5.3 %collective-permute-start.21 = (bf16[96,4224]{1,0:T(8,128)(2,1)}, bf16[96,4224]{1,0:T(8,128)(2,1)S(1)}, u32[]{:S(2)}, u32[]{:S(2)}) collective-permute-start(bf16[96,4224]{1,0:T(8,128)(2,1)} %get-tuple-element.92), channel_id=1, source_target_pairs={{0,8},{8,0},{16,24},{24,16},{1,9},{9,1},{17,25},{25,17},{2,10},{10... | collective-permute-start | bytes 2433032 | tf_op jit(solution)/shard_map/ppermute | solution.py:455
  330.7 0.7 collective-permute-start.23
  331.4 12.9 %collective-permute-done.19.refs_5_.refs_13_ = bf16[48,8320]{1,0:T(8,128)(2,1)S(1)} collective-permute-done((bf16[48,8320]{1,0:T(8,128)(2,1)}, bf16[48,8320]{1,0:T(8,128)(2,1)S(1)}, u32[]{:S(2)}, u32[]{:S(2)}) %collective-permute-start.19) | collective-permute-done | bytes 798752 | tf_op jit(solution)/shard_map/ppermute | solution.py:458
  344.3 2.7 collective-permute-start.24
  347.0 28.7 %shard_map.117 = (bf16[192,1792]{1,0:T(8,128)(2,1)}, bf16[192,1792]{1,0:T(8,128)(2,1)}, bf16[192,1792]{1,0:T(8,128)(2,1)}, bf16[192,4096]{1,0:T(8,128)(2,1)}, bf...) custom-call(s32[1]{0:T(128)} %bitcast.3.refs_0_, ...), custom_call_target="tpu_custom_call", output_to_operand_aliasing={{6}: (9, {})} | custom-call | tf_op jit(solution)/shard_map/pallas_call | solution.py:75
  375.7 1.4 collective-permute-start.20
  377.1 25.2 %shard_map.118 = (bf16[96,1792]{1,0:T(8,128)(2,1)}, bf16[96,1792]{1,0:T(8,128)(2,1)}, bf16[96,1792]{1,0:T(8,128)(2,1)}, bf16[96,4096]{1,0:T(8,128)(2,1)}, bf16[4...) custom-call(s32[1]{0:T(128)} %bitcast.3.refs_0_, ...), custom_call_target="tpu_custom_call", output_to_operand_aliasing={{6}: (7, {})} | custom-call | tf_op jit(solution)/shard_map/pallas_call | solution.py:75
  402.3 0.9 collective-permute-start.30
  403.2 0.8 copy-done.13
  404.9 4.2 shard_map.119
  409.1 1.2 collective-permute-start.26
  410.3 2.6 collective-permute-start.27
  412.9 0.7 collective-permute-start.28
  413.6 5.1 %collective-permute-start.29 = (bf16[48,4224]{1,0:T(8,128)(2,1)}, bf16[48,4224]{1,0:T(8,128)(2,1)S(1)}, u32[]{:S(2)}, u32[]{:S(2)}) collective-permute-start(bf16[48,4224]{1,0:T(8,128)(2,1)} %get-tuple-element.104), channel_id=1, source_target_pairs={{0,24},{24,0},{1,25},{25,1},{2,26},{26,2},{3,27},{27,3},{4,28},{28... | collective-permute-start | bytes 1216520 | tf_op jit(solution)/shard_map/ppermute | solution.py:455
  418.7 18.2 %shard_map.120 = (bf16[1792,4096]{1,0:T(8,128)(2,1)}, f32[8,128]{1,0:T(8,128)}) custom-call(bf16[192,4096]{1,0:T(8,128)(2,1)} %get-tuple-element.107.refs_0_, bf16[288,4096]{1,0:T(8,128)(2,1)} %get-tuple-element.108.refs_1_, bf16[192,4096]{1,0:T(8,128)(2,1)} %get-tuple-element.109.refs_2_, ...), custom_call_target="tpu_custom_call", output_to_operand_aliasing={{1}: (8, {})} | custom-call | tf_op jit(solution)/shard_map/pallas_call | solution.py:75
  436.9 0.7 copy-done.22
  437.6 2.0 shard_map.121
  439.6 18.5 %shard_map.122 = (bf16[1792,4096]{1,0:T(8,128)(2,1)}, f32[8,128]{1,0:T(8,128)}) custom-call(bf16[48,8320]{1,0:T(8,128)(2,1)} %copy-done.8, bf16[48,8320]{1,0:T(8,128)(2,1)} %collective-permute-done.6.refs_3_.refs_1_, bf16[48,8320]{1,0:T(8,128)(2,1)} %copy-done.2, ...), custom_call_target="tpu_custom_call", output_to_operand_aliasing={{1}: (20, {})} | custom-call | tf_op jit(solution)/shard_map/pallas_call | solution.py:75
  458.2 0.7 copy-done.27
  459.4 3.0 shard_map.123
  462.4 1.2 collective-permute-start.34
  463.6 1.6 collective-permute-start.32
  465.2 1.9 collective-permute-start.35
  467.2 0.8 collective-permute-start.33
  467.9 18.5 %shard_map.124 = (bf16[1792,4096]{1,0:T(8,128)(2,1)}, f32[8,128]{1,0:T(8,128)}) custom-call(bf16[48,8320]{1,0:T(8,128)(2,1)} %copy-done.8, bf16[48,8320]{1,0:T(8,128)(2,1)} %collective-permute-done.6.refs_3_.refs_1_, bf16[48,8320]{1,0:T(8,128)(2,1)} %copy-done.2, ...), custom_call_target="tpu_custom_call", output_to_operand_aliasing={{1}: (20, {})} | custom-call | tf_op jit(solution)/shard_map/pallas_call | solution.py:75
  486.5 0.6 collective-permute-done.33.refs_2_
  487.8 3.7 shard_map.125
  491.5 1.5 reduce.1
  (96 shorter events, 4.6 us)
Async XLA Ops:
  3.8 1.2 copy-start
  5.1 1.2 copy-start.1
  7.6 0.7 collective-permute-start
  8.3 27.9 %copy-start.8 = (bf16[48,8320]{1,0:T(8,128)(2,1)}, bf16[48,8320]{1,0:T(8,128)(2,1)S(1)}, u32[]{:S(2)}) copy-start(bf16[48,8320]{1,0:T(8,128)(2,1)S(1)} %collective-permute-done.refs_2_.refs_0_) | copy-start | bytes 2396164
  8.3 20.9 %collective-permute-start.8 = (bf16[48,8320]{1,0:T(8,128)(2,1)S(1)}, bf16[48,8320]{1,0:T(8,128)(2,1)S(1)}, u32[]{:S(2)}, u32[]{:S(2)}) collective-permute-start(bf16[48,8320]{1,0:T(8,128)(2,1)S(1)} %collective-permute-done.refs_2_.refs_0_), channel_id=1, source_target_pairs={{0,8},{8,0},{16,24},{24,16},{1,9},{9,1},{17,25},{25,17},{2,10},{10... | collective-permute-start | bytes 2396168 | tf_op jit(solution)/shard_map/ppermute | solution.py:455
  11.4 21.1 %collective-permute-start.1 = (bf16[48,8320]{1,0:T(8,128)(2,1)S(1)}, bf16[48,8320]{1,0:T(8,128)(2,1)}, u32[]{:S(2)}, u32[]{:S(2)}) collective-permute-start(bf16[48,8320]{1,0:T(8,128)(2,1)S(1)} %collective-permute-done.refs_2_.refs_0_), channel_id=1, source_target_pairs={{8,16},{16,8},{9,17},{17,9},{10,18},{18,10},{11,19},{19,11},{12,20... | collective-permute-start | bytes 2396168 | tf_op jit(solution)/shard_map/ppermute | solution.py:455
  29.2 7.0 %copy-start.4 = (bf16[48,8320]{1,0:T(8,128)(2,1)}, bf16[48,8320]{1,0:T(8,128)(2,1)S(1)}, u32[]{:S(2)}) copy-start(bf16[48,8320]{1,0:T(8,128)(2,1)S(1)} %collective-permute-done.8.refs_2_.refs_4_) | copy-start | bytes 2396164
  29.2 7.0 %collective-permute-start.9 = (bf16[48,8320]{1,0:T(8,128)(2,1)S(1)}, bf16[48,8320]{1,0:T(8,128)(2,1)}, u32[]{:S(2)}, u32[]{:S(2)}) collective-permute-start(bf16[48,8320]{1,0:T(8,128)(2,1)S(1)} %collective-permute-done.8.refs_2_.refs_4_), channel_id=1, source_target_pairs={{8,16},{16,8},{9,17},{17,9},{10,18},{18,10},{11,19},{19,11},{12,20... | collective-permute-start | bytes 2396168 | tf_op jit(solution)/shard_map/ppermute | solution.py:455
  30.8 20.7 %collective-permute-start.3 = (bf16[48,8320]{1,0:T(8,128)(2,1)S(1)}, bf16[48,8320]{1,0:T(8,128)(2,1)S(1)}, u32[]{:S(2)}, u32[]{:S(2)}) collective-permute-start(bf16[48,8320]{1,0:T(8,128)(2,1)S(1)} %get-tuple-element.72), channel_id=1, source_target_pairs={{0,4},{1,7},{2,6},{3,5},{4,0},{5,3},{6,2},{7,1},{8,12},{9,15},{10,... | collective-permute-start | bytes 2396168 | tf_op jit(solution)/shard_map/ppermute | solution.py:452
  32.5 23.3 %collective-permute-start.2 = (bf16[48,8320]{1,0:T(8,128)(2,1)}, bf16[48,8320]{1,0:T(8,128)(2,1)}, u32[]{:S(2)}, u32[]{:S(2)}) collective-permute-start(bf16[48,8320]{1,0:T(8,128)(2,1)} %collective-permute-done.1.refs_1_), channel_id=1, source_target_pairs={{8,0},{16,24},{9,1},{17,25},{10,2},{18,26},{11,3},{19,27},{12,4},{... | collective-permute-start | bytes 2396168 | tf_op jit(solution)/shard_map/ppermute | solution.py:455
  33.7 78.1 %collective-permute-start.6 = (bf16[48,8320]{1,0:T(8,128)(2,1)S(1)}, bf16[48,8320]{1,0:T(8,128)(2,1)}, u32[]{:S(2)}, u32[]{:S(2)}) collective-permute-start(bf16[48,8320]{1,0:T(8,128)(2,1)S(1)} %get-tuple-element.74), channel_id=1, source_target_pairs={{0,2},{1,1},{2,0},{3,3},{4,6},{5,5},{6,4},{7,7},{8,10},{9,9},{10,8... | collective-permute-start | bytes 2396168 | tf_op jit(solution)/shard_map/ppermute | solution.py:452
  35.7 80.6 %collective-permute-start.7 = (bf16[48,8320]{1,0:T(8,128)(2,1)S(1)}, bf16[48,8320]{1,0:T(8,128)(2,1)}, u32[]{:S(2)}, u32[]{:S(2)}) collective-permute-start(bf16[48,8320]{1,0:T(8,128)(2,1)S(1)} %get-tuple-element.75), channel_id=1, source_target_pairs={{0,6},{1,5},{2,4},{3,7},{4,2},{5,1},{6,0},{7,3},{8,14},{9,13},{10,... | collective-permute-start | bytes 2396168 | tf_op jit(solution)/shard_map/ppermute | solution.py:452
  36.2 108.5 %collective-permute-start.10 = (bf16[48,8320]{1,0:T(8,128)(2,1)}, bf16[48,8320]{1,0:T(8,128)(2,1)}, u32[]{:S(2)}, u32[]{:S(2)}) collective-permute-start(bf16[48,8320]{1,0:T(8,128)(2,1)} %collective-permute-done.9.refs_1_), channel_id=1, source_target_pairs={{8,0},{16,24},{9,1},{17,25},{10,2},{18,26},{11,3},{19,27},{12,4},{... | collective-permute-start | bytes 2396168 | tf_op jit(solution)/shard_map/ppermute | solution.py:455
  51.5 4.9 copy-start.2
  105.9 90.4 %collective-permute-start.5 = (bf16[48,8320]{1,0:T(8,128)(2,1)}, bf16[48,8320]{1,0:T(8,128)(2,1)S(1)}, u32[]{:S(2)}, u32[]{:S(2)}) collective-permute-start(bf16[48,8320]{1,0:T(8,128)(2,1)} %get-tuple-element.73), channel_id=1, source_target_pairs={{0,24},{24,0},{1,25},{25,1},{2,26},{26,2},{3,27},{27,3},{4,28},{28... | collective-permute-start | bytes 2396168 | tf_op jit(solution)/shard_map/ppermute | solution.py:455
  110.5 85.8 %collective-permute-start.4 = (bf16[48,8320]{1,0:T(8,128)(2,1)}, bf16[48,8320]{1,0:T(8,128)(2,1)S(1)}, u32[]{:S(2)}, u32[]{:S(2)}) collective-permute-start(bf16[48,8320]{1,0:T(8,128)(2,1)} %get-tuple-element.73), channel_id=1, source_target_pairs={{0,16},{24,8},{1,17},{25,9},{2,18},{26,10},{3,19},{27,11},{4,20},{... | collective-permute-start | bytes 2396168 | tf_op jit(solution)/shard_map/ppermute | solution.py:455
  111.8 123.4 %collective-permute-start.16 = (bf16[48,8320]{1,0:T(8,128)(2,1)}, bf16[48,8320]{1,0:T(8,128)(2,1)S(1)}, u32[]{:S(2)}, u32[]{:S(2)}) collective-permute-start(bf16[48,8320]{1,0:T(8,128)(2,1)} %copy-done.4), channel_id=1, source_target_pairs={{0,1},{1,0},{2,3},{3,2},{4,5},{5,4},{6,7},{7,6},{8,9},{9,8},{10,11... | collective-permute-start | bytes 2396168 | tf_op jit(solution)/shard_map/ppermute | solution.py:458
  116.2 120.3 %collective-permute-start.17 = (bf16[48,8320]{1,0:T(8,128)(2,1)}, bf16[48,8320]{1,0:T(8,128)(2,1)S(1)}, u32[]{:S(2)}, u32[]{:S(2)}) collective-permute-start(bf16[48,8320]{1,0:T(8,128)(2,1)} %get-tuple-element.83.refs_4_.refs_6_), channel_id=1, source_target_pairs={{0,1},{1,0},{2,3},{3,2},{4,5},{5,4},{6,7},{7,6},{8,9},{9,8},{10,11... | collective-permute-start | bytes 2396168 | tf_op jit(solution)/shard_map/ppermute | solution.py:458
  194.3 43.2 %collective-permute-start.18 = (bf16[48,8320]{1,0:T(8,128)(2,1)}, bf16[48,8320]{1,0:T(8,128)(2,1)S(1)}, u32[]{:S(2)}, u32[]{:S(2)}) collective-permute-start(bf16[48,8320]{1,0:T(8,128)(2,1)} %get-tuple-element.84.refs_6_.refs_8_), channel_id=1, source_target_pairs={{0,1},{1,0},{2,3},{3,2},{4,5},{5,4},{6,7},{7,6},{8,9},{9,8},{10,11... | collective-permute-start | bytes 2396168 | tf_op jit(solution)/shard_map/ppermute | solution.py:458
  196.3 0.9 copy-start.17
  196.3 1.1 copy-start.18
  235.0 36.8 %collective-permute-start.14 = (bf16[48,8320]{1,0:T(8,128)(2,1)}, bf16[48,8320]{1,0:T(8,128)(2,1)S(1)}, u32[]{:S(2)}, u32[]{:S(2)}) collective-permute-start(bf16[48,8320]{1,0:T(8,128)(2,1)} %get-tuple-element.80.refs_2_.refs_10_), channel_id=1, source_target_pairs={{0,1},{1,0},{2,3},{3,2},{4,5},{5,4},{6,7},{7,6},{8,9},{9,8},{10,11... | collective-permute-start | bytes 2396168 | tf_op jit(solution)/shard_map/ppermute | solution.py:458
  235.2 36.7 %collective-permute-start.13 = (bf16[48,8320]{1,0:T(8,128)(2,1)}, bf16[48,8320]{1,0:T(8,128)(2,1)S(1)}, u32[]{:S(2)}, u32[]{:S(2)}) collective-permute-start(bf16[48,8320]{1,0:T(8,128)(2,1)} %get-tuple-element.81), channel_id=1, source_target_pairs={{0,8},{8,0},{16,24},{24,16},{1,9},{9,1},{17,25},{25,17},{2,10},{10... | collective-permute-start | bytes 2396168 | tf_op jit(solution)/shard_map/ppermute | solution.py:455
  235.2 4.2 copy-start.5
  235.2 36.7 %collective-permute-start.12 = (bf16[48,8320]{1,0:T(8,128)(2,1)}, bf16[48,8320]{1,0:T(8,128)(2,1)S(1)}, u32[]{:S(2)}, u32[]{:S(2)}) collective-permute-start(bf16[48,8320]{1,0:T(8,128)(2,1)} %get-tuple-element.81), channel_id=1, source_target_pairs={{16,0},{8,24},{17,1},{9,25},{18,2},{10,26},{19,3},{11,27},{20,4},{... | collective-permute-start | bytes 2396168 | tf_op jit(solution)/shard_map/ppermute | solution.py:455
  236.5 2.9 copy-start.6
  236.5 35.4 %collective-permute-start.11 = (bf16[48,8320]{1,0:T(8,128)(2,1)}, bf16[48,8320]{1,0:T(8,128)(2,1)S(1)}, u32[]{:S(2)}, u32[]{:S(2)}) collective-permute-start(bf16[48,8320]{1,0:T(8,128)(2,1)} %get-tuple-element.81), channel_id=1, source_target_pairs={{8,16},{16,8},{9,17},{17,9},{10,18},{18,10},{11,19},{19,11},{12,20... | collective-permute-start | bytes 2396168 | tf_op jit(solution)/shard_map/ppermute | solution.py:455
  237.4 2.0 copy-start.7
  237.4 34.4 %collective-permute-start.15 = (bf16[48,4224]{1,0:T(8,128)(2,1)}, bf16[48,4224]{1,0:T(8,128)(2,1)S(1)}, u32[]{:S(2)}, u32[]{:S(2)}) collective-permute-start(bf16[48,4224]{1,0:T(8,128)(2,1)} %get-tuple-element.82), channel_id=1, source_target_pairs={{0,1},{1,0},{2,3},{3,2},{4,5},{5,4},{6,7},{7,6},{8,9},{9,8},{10,11... | collective-permute-start | bytes 1216520 | tf_op jit(solution)/shard_map/ppermute | solution.py:458
  271.9 1.0 copy-start.3
  271.9 1.3 copy-start.19
  271.9 1.6 copy-start.20
  271.9 1.8 copy-start.21
  323.3 21.0 %collective-permute-start.19 = (bf16[48,8320]{1,0:T(8,128)(2,1)}, bf16[48,8320]{1,0:T(8,128)(2,1)S(1)}, u32[]{:S(2)}, u32[]{:S(2)}) collective-permute-start(bf16[48,8320]{1,0:T(8,128)(2,1)} %get-tuple-element.87.refs_3_.refs_11_), channel_id=1, source_target_pairs={{0,1},{1,0},{2,3},{3,2},{4,5},{5,4},{6,7},{7,6},{8,9},{9,8},{10,11... | collective-permute-start | bytes 2396168 | tf_op jit(solution)/shard_map/ppermute | solution.py:458
  324.3 51.3 %collective-permute-start.25 = (bf16[48,8320]{1,0:T(8,128)(2,1)}, bf16[48,8320]{1,0:T(8,128)(2,1)S(1)}, u32[]{:S(2)}, u32[]{:S(2)}) collective-permute-start(bf16[48,8320]{1,0:T(8,128)(2,1)} %get-tuple-element.96.refs_2_.refs_14_), channel_id=1, source_target_pairs={{0,1},{1,0},{2,3},{3,2},{4,5},{5,4},{6,7},{7,6},{8,9},{9,8},{10,11... | collective-permute-start | bytes 2396168 | tf_op jit(solution)/shard_map/ppermute | solution.py:458
  325.3 76.9 %collective-permute-start.21 = (bf16[96,4224]{1,0:T(8,128)(2,1)}, bf16[96,4224]{1,0:T(8,128)(2,1)S(1)}, u32[]{:S(2)}, u32[]{:S(2)}) collective-permute-start(bf16[96,4224]{1,0:T(8,128)(2,1)} %get-tuple-element.92), channel_id=1, source_target_pairs={{0,8},{8,0},{16,24},{24,16},{1,9},{9,1},{17,25},{25,17},{2,10},{10... | collective-permute-start | bytes 2433032 | tf_op jit(solution)/shard_map/ppermute | solution.py:455
  330.7 72.4 %collective-permute-start.22 = (bf16[96,4224]{1,0:T(8,128)(2,1)}, bf16[96,4224]{1,0:T(8,128)(2,1)S(1)}, u32[]{:S(2)}, u32[]{:S(2)}) collective-permute-start(bf16[96,4224]{1,0:T(8,128)(2,1)} %get-tuple-element.93), channel_id=1, source_target_pairs={{0,16},{16,0},{8,24},{24,8},{1,17},{17,1},{9,25},{25,9},{2,18},{18... | collective-permute-start | bytes 2433032 | tf_op jit(solution)/shard_map/ppermute | solution.py:455
  330.7 72.4 %collective-permute-start.23 = (bf16[96,4224]{1,0:T(8,128)(2,1)}, bf16[96,4224]{1,0:T(8,128)(2,1)S(1)}, u32[]{:S(2)}, u32[]{:S(2)}) collective-permute-start(bf16[96,4224]{1,0:T(8,128)(2,1)} %get-tuple-element.94), channel_id=1, source_target_pairs={{8,16},{16,8},{9,17},{17,9},{10,18},{18,10},{11,19},{19,11},{12,20... | collective-permute-start | bytes 2433032 | tf_op jit(solution)/shard_map/ppermute | solution.py:455
  344.3 2.7 copy-start.9
  344.3 58.9 %collective-permute-start.24 = (bf16[96,4224]{1,0:T(8,128)(2,1)}, bf16[96,4224]{1,0:T(8,128)(2,1)S(1)}, u32[]{:S(2)}, u32[]{:S(2)}) collective-permute-start(bf16[96,4224]{1,0:T(8,128)(2,1)} %get-tuple-element.95), channel_id=1, source_target_pairs={{0,24},{24,0},{1,25},{25,1},{2,26},{26,2},{3,27},{27,3},{4,28},{28... | collective-permute-start | bytes 2433032 | tf_op jit(solution)/shard_map/ppermute | solution.py:455
  375.7 1.4 copy-start.10
  375.7 27.5 %collective-permute-start.20 = (bf16[96,4224]{1,0:T(8,128)(2,1)}, bf16[96,4224]{1,0:T(8,128)(2,1)S(1)}, u32[]{:S(2)}, u32[]{:S(2)}) collective-permute-start(bf16[96,4224]{1,0:T(8,128)(2,1)} %get-tuple-element.90), channel_id=1, source_target_pairs={{0,1},{1,0},{2,3},{3,2},{4,5},{5,4},{6,7},{7,6},{8,9},{9,8},{10,11... | collective-permute-start | bytes 2433032 | tf_op jit(solution)/shard_map/ppermute | solution.py:458
  402.2 1.0 copy-start.12
  402.3 34.6 %collective-permute-start.30 = (bf16[48,4224]{1,0:T(8,128)(2,1)}, bf16[48,4224]{1,0:T(8,128)(2,1)S(1)}, u32[]{:S(2)}, u32[]{:S(2)}) collective-permute-start(bf16[48,4224]{1,0:T(8,128)(2,1)} %get-tuple-element.106), channel_id=1, source_target_pairs={{0,1},{1,0},{2,3},{3,2},{4,5},{5,4},{6,7},{7,6},{8,9},{9,8},{10,11... | collective-permute-start | bytes 1216520 | tf_op jit(solution)/shard_map/ppermute | solution.py:458
  403.1 0.9 copy-start.13
  403.2 1.2 copy-start.14
  403.2 1.4 copy-start.15
  403.2 1.7 copy-start.16
  409.1 49.0 %collective-permute-start.26 = (bf16[48,4224]{1,0:T(8,128)(2,1)}, bf16[48,4224]{1,0:T(8,128)(2,1)S(1)}, u32[]{:S(2)}, u32[]{:S(2)}) collective-permute-start(bf16[48,4224]{1,0:T(8,128)(2,1)} %get-tuple-element.100), channel_id=1, source_target_pairs={{0,1},{1,0},{2,3},{3,2},{4,5},{5,4},{6,7},{7,6},{8,9},{9,8},{10,11... | collective-permute-start | bytes 1216520 | tf_op jit(solution)/shard_map/ppermute | solution.py:458
  410.3 47.8 %collective-permute-start.27 = (bf16[48,4224]{1,0:T(8,128)(2,1)}, bf16[48,4224]{1,0:T(8,128)(2,1)S(1)}, u32[]{:S(2)}, u32[]{:S(2)}) collective-permute-start(bf16[48,4224]{1,0:T(8,128)(2,1)} %get-tuple-element.102), channel_id=1, source_target_pairs={{0,16},{16,0},{8,24},{24,8},{1,17},{17,1},{9,25},{25,9},{2,18},{18... | collective-permute-start | bytes 1216520 | tf_op jit(solution)/shard_map/ppermute | solution.py:455
  412.9 45.3 %collective-permute-start.28 = (bf16[48,4224]{1,0:T(8,128)(2,1)}, bf16[48,4224]{1,0:T(8,128)(2,1)S(1)}, u32[]{:S(2)}, u32[]{:S(2)}) collective-permute-start(bf16[48,4224]{1,0:T(8,128)(2,1)} %get-tuple-element.103), channel_id=1, source_target_pairs={{8,16},{16,8},{9,17},{17,9},{10,18},{18,10},{11,19},{19,11},{12,20... | collective-permute-start | bytes 1216520 | tf_op jit(solution)/shard_map/ppermute | solution.py:455
  413.6 44.6 %collective-permute-start.29 = (bf16[48,4224]{1,0:T(8,128)(2,1)}, bf16[48,4224]{1,0:T(8,128)(2,1)S(1)}, u32[]{:S(2)}, u32[]{:S(2)}) collective-permute-start(bf16[48,4224]{1,0:T(8,128)(2,1)} %get-tuple-element.104), channel_id=1, source_target_pairs={{0,24},{24,0},{1,25},{25,1},{2,26},{26,2},{3,27},{27,3},{4,28},{28... | collective-permute-start | bytes 1216520 | tf_op jit(solution)/shard_map/ppermute | solution.py:455
  439.6 18.6 %collective-permute-start.31 = (bf16[48,4224]{1,0:T(8,128)(2,1)}, bf16[48,4224]{1,0:T(8,128)(2,1)S(1)}, u32[]{:S(2)}, u32[]{:S(2)}) collective-permute-start(bf16[48,4224]{1,0:T(8,128)(2,1)} %get-tuple-element.117), channel_id=1, source_target_pairs={{0,8},{8,0},{16,24},{24,16},{1,9},{9,1},{17,25},{25,17},{2,10},{10... | collective-permute-start | bytes 1216520 | tf_op jit(solution)/shard_map/ppermute | solution.py:455
  458.1 0.9 copy-start.28
  458.1 1.0 copy-start.29
  458.2 1.1 copy-start.30
  458.2 1.2 copy-start.31
  462.4 24.0 %collective-permute-start.34 = (bf16[48,4224]{1,0:T(8,128)(2,1)}, bf16[48,4224]{1,0:T(8,128)(2,1)S(1)}, u32[]{:S(2)}, u32[]{:S(2)}) collective-permute-start(bf16[48,4224]{1,0:T(8,128)(2,1)} %get-tuple-element.124), channel_id=1, source_target_pairs={{0,1},{1,2},{2,3},{3,0},{4,5},{5,6},{6,7},{7,4},{8,9},{9,10},{10,1... | collective-permute-start | bytes 1216520 | tf_op jit(solution)/shard_map/ppermute | solution.py:452
  463.6 22.9 %collective-permute-start.32 = (bf16[48,4224]{1,0:T(8,128)(2,1)}, bf16[48,4224]{1,0:T(8,128)(2,1)S(1)}, u32[]{:S(2)}, u32[]{:S(2)}) collective-permute-start(bf16[48,4224]{1,0:T(8,128)(2,1)} %get-tuple-element.124), channel_id=1, source_target_pairs={{0,0},{1,3},{2,2},{3,1},{4,4},{5,7},{6,6},{7,5},{8,8},{9,11},{10,1... | collective-permute-start | bytes 1216520 | tf_op jit(solution)/shard_map/ppermute | solution.py:452
  465.2 21.2 %collective-permute-start.35 = (bf16[48,4224]{1,0:T(8,128)(2,1)}, bf16[48,4224]{1,0:T(8,128)(2,1)S(1)}, u32[]{:S(2)}, u32[]{:S(2)}) collective-permute-start(bf16[48,4224]{1,0:T(8,128)(2,1)} %get-tuple-element.125), channel_id=1, source_target_pairs={{0,5},{1,6},{2,7},{3,4},{4,1},{5,2},{6,3},{7,0},{8,13},{9,14},{10,... | collective-permute-start | bytes 1216520 | tf_op jit(solution)/shard_map/ppermute | solution.py:452
  467.2 19.9 %collective-permute-start.33 = (bf16[48,4224]{1,0:T(8,128)(2,1)}, bf16[48,4224]{1,0:T(8,128)(2,1)S(1)}, u32[]{:S(2)}, u32[]{:S(2)}) collective-permute-start(bf16[48,4224]{1,0:T(8,128)(2,1)} %get-tuple-element.125), channel_id=1, source_target_pairs={{0,4},{1,7},{2,6},{3,5},{4,0},{5,3},{6,2},{7,1},{8,12},{9,15},{10,... | collective-permute-start | bytes 1216520 | tf_op jit(solution)/shard_map/ppermute | solution.py:452
  486.4 0.8 copy-start.23
  486.4 0.9 copy-start.24
  486.5 1.0 copy-start.25
  (4 other events, 3.0 us)

commit v2 on v1

--- a/solution.py
+++ b/solution.py
@@ -13,14 +13,9 @@
 VMEM = 56 * MIB
 SMALL = pl.CostEstimate(flops=0, bytes_accessed=0, transcendentals=0)
 
-OUTER = ((0, 1), (1, 0), (2, 3), (3, 2))
+PAIRS = [[(i, i ^ k) for i in range(4)] for k in range(4)]
 MIDDLE = ((1, 2), (2, 1))
 OUT = ((1, 0), (2, 3))
-IN = ((0, 1), (3, 2))
-SKIP = ((0, 2), (2, 0), (1, 3), (3, 1))
-ENDS = ((0, 3), (3, 0))
-IN_TWO = ((0, 2), (3, 1))
-OUT_TWO = ((2, 0), (1, 3))
 
 
 def nt_dot(a, b):
@@ -31,12 +26,31 @@
     return lax.dot_general(a, b, (((0,), (0,)), ((), ())), preferred_element_type=jnp.float32)
 
 
-def pack_kernel(slot_ref, rows_ref, grads_ref, scale_ref, *out_refs):
+def pack_kernel(e_ref, x_ref, across_ref, down_ref, rows_in, grads_in, scale_ref, *refs):
+    slot_out, out_refs = refs[0], refs[1:5]
+    rows_ref, grads_ref, sems = refs[5:]
     width = rows_ref.shape[1]
-    slot = slot_ref[...]
+    copies = [
+        pltpu.make_async_copy(a, b, sems.at[i])
+        for i, (a, b) in enumerate(((rows_in, rows_ref), (grads_in, grads_ref)))
+    ]
+    for copy in copies:
+        copy.start()
+    count = rows_ref.shape[0]
+    size = out_refs[0].shape[0]
+    route = across_ref[...]
+    earlier = lax.broadcasted_iota(jnp.int32, (count, count), 0) < lax.broadcasted_iota(
+        jnp.int32, (count, count), 1
+    )
+    same = (down_ref[...] == route) & earlier
+    rank = jnp.sum(same.astype(jnp.int32), axis=0, keepdims=True)
+    other = lax.bitwise_xor(route, e_ref[0])
+    slot = (lax.bitwise_xor(other & 1, x_ref[0]) * 2 + (other >> 1)) * size + rank
+    slot_out[...] = slot
+    for copy in copies:
+        copy.wait()
     for group, out_ref in enumerate(out_refs):
-        size = out_ref.shape[0]
-        at = lax.broadcasted_iota(jnp.int32, (size, slot.shape[1]), 0) + group * size
+        at = lax.broadcasted_iota(jnp.int32, (size, count), 0) + group * size
         placing = (at == slot).astype(jnp.float32).astype(jnp.bfloat16)
         for start, ref in ((0, rows_ref), (width, grads_ref), (2 * width, scale_ref)):
             out_ref[:, start : start + ref.shape[1]] = jnp.dot(
@@ -44,19 +58,29 @@
             ).astype(jnp.bfloat16)
 
 
-def pack(slot, rows, grads, scale, groups, size):
-    width = rows.shape[1]
-    shape = jax.ShapeDtypeStruct((size, 2 * width + LANES), jnp.bfloat16)
+def pack(e, x, routing, rows, grads, scale, size):
+    count, width = rows.shape
+    scalar = pl.BlockSpec(memory_space=pltpu.SMEM)
+    inside = pl.BlockSpec(memory_space=pltpu.VMEM)
+    anywhere = pl.BlockSpec(memory_space=pl.ANY)
     return pl.pallas_call(
         pack_kernel,
-        out_shape=[shape] * groups,
-        compiler_params=pltpu.CompilerParams(vmem_limit_bytes=32 * MIB),
-        cost_estimate=pl.CostEstimate(
-            flops=2 * groups * size * rows.shape[0] * 2 * width,
-            bytes_accessed=4 * (rows.shape[0] + groups * size) * width,
-            transcendentals=0,
-        ),
-    )(slot, rows, grads, scale)
+        in_specs=[scalar, scalar, inside, inside, anywhere, anywhere, inside],
+        out_specs=[inside] * 5,
+        out_shape=[jax.ShapeDtypeStruct((1, count), jnp.int32)]
+        + [jax.ShapeDtypeStruct((size, 2 * width + LANES), jnp.bfloat16)] * 4,
+        scratch_shapes=[
+            pltpu.VMEM((count, width), jnp.bfloat16),
+            pltpu.VMEM((count, width), jnp.bfloat16),
+            pltpu.SemaphoreType.DMA((2,)),
+        ],
+        compiler_params=pltpu.CompilerParams(vmem_limit_bytes=VMEM),
+        cost_estimate=SMALL,
+    )(e, x, routing.reshape(1, count), routing, rows, grads, scale)
+
+
+def nothing_kernel(*refs):
+    del refs
 
 
 class Order:
@@ -84,75 +108,62 @@
         )(*operands, self.token)
         return out
 
+    def wait(self, *arrays):
+        self.call(nothing_kernel, arrays, [pl.BlockSpec(memory_space=pl.ANY)] * len(arrays), [], [])
+
 
 def choose_kernel(picks, copies, needs, flag_ref, *refs):
     n_in = 2 * picks + copies
-    ins, outs = refs[:n_in], refs[n_in + needs : -1]
-    sems = refs[-1]
+    ins, outs = refs[:n_in], refs[n_in + needs :]
 
     def move(first):
-        pairs = [(ins[2 * i + 1 - first], outs[i]) for i in range(picks)]
-        pairs += [(ins[2 * picks + i], outs[picks + i]) for i in range(copies)]
-        moves = [pltpu.make_async_copy(a, b, sems.at[i]) for i, (a, b) in enumerate(pairs)]
-        for one in moves:
-            one.start()
-        for one in moves:
-            one.wait()
-
-    @pl.when(flag_ref[0] == 1)
-    def _():
-        move(1)
-
-    @pl.when(flag_ref[0] != 1)
-    def _():
-        move(0)
+        for i in range(picks):
+            outs[i][...] = ins[2 * i + 1 - first][...]
+
+    pl.when(flag_ref[0] == 1)(functools.partial(move, 1))
+    pl.when(flag_ref[0] != 1)(functools.partial(move, 0))
+    for i in range(copies):
+        outs[picks + i][...] = ins[2 * picks + i][...]
 
 
 def choose(order, flag, pairs, singles=(), needs=()):
-    operands = [flag, *[a for pair in pairs for a in pair], *singles, *needs]
-    anywhere = pl.BlockSpec(memory_space=pl.ANY)
+    moved = [*[a for pair in pairs for a in pair], *singles]
+    inside = pl.BlockSpec(memory_space=pltpu.VMEM)
     out_shape = [jax.ShapeDtypeStruct(a.shape, a.dtype) for a in [p[0] for p in pairs] + list(singles)]
     return order.call(
         functools.partial(choose_kernel, len(pairs), len(singles), len(needs)),
-        operands,
-        [pl.BlockSpec(memory_space=pltpu.SMEM)] + [anywhere] * (len(operands) - 1),
+        [flag, *moved, *needs],
+        [pl.BlockSpec(memory_space=pltpu.SMEM)]
+        + [inside] * len(moved)
+        + [pl.BlockSpec(memory_space=pl.ANY)] * len(needs),
         out_shape,
-        [anywhere] * len(out_shape),
-        scratch_shapes=[pltpu.SemaphoreType.DMA((len(out_shape),))],
-    )
-
-
-def sum_kernel(plan, flag_ref, *refs):
-    n_in = len(refs) - len(plan)
-    for (rows, terms, others), out_ref in zip(plan, refs[n_in:], strict=True):
-
-        def add(terms, out_ref=out_ref, rows=rows):
+        [inside] * len(out_shape),
+    )
+
+
+def sum_kernel(plan, size, *refs):
+    for pieces, out_ref in zip(plan, refs[len(refs) - len(plan) :], strict=True):
+        for i, terms in enumerate(pieces):
             total = None
             for k, start in terms:
-                term = refs[k][start : start + rows, :].astype(jnp.float32)
+                term = refs[k][start : start + size, :].astype(jnp.float32)
                 total = term if total is None else total + term
-            out_ref[...] = total.astype(out_ref.dtype)
-
-        if others is None:
-            add(terms)
-        else:
-            pl.when(flag_ref[0] == 1)(functools.partial(add, terms))
-            pl.when(flag_ref[0] != 1)(functools.partial(add, others))
-
-
-def sums(order, flag, operands, plan):
+            out_ref[i * size : (i + 1) * size, :] = total.astype(out_ref.dtype)
+
+
+def sums(order, operands, size, *plan):
     width = operands[0].shape[1]
     inside = pl.BlockSpec(memory_space=pltpu.VMEM)
     return order.call(
-        functools.partial(sum_kernel, plan),
-        [flag, *operands],
-        [pl.BlockSpec(memory_space=pltpu.SMEM)] + [inside] * len(operands),
-        [jax.ShapeDtypeStruct((rows, width), jnp.bfloat16) for rows, _, _ in plan],
+        functools.partial(sum_kernel, plan, size),
+        operands,
+        [inside] * len(operands),
+        [jax.ShapeDtypeStruct((size * len(pieces), width), jnp.bfloat16) for pieces in plan],
         [inside] * len(plan),
     )
 
 
-def unit_kernel(n_pieces, parts, count, lane_ref, flag_ref, *refs):
+def unit_kernel(n_pieces, parts, count, lane_ref, *refs):
     pieces = refs[:n_pieces]
     weights = refs[n_pieces : n_pieces + 3]
     refs = refs[n_pieces + 3 :]
@@ -289,13 +300,10 @@
     lax.fori_loop(1, count, step, 0)
 
     def write(at, value):
-        for ref, (start, size, other) in zip(partial_refs, parts, strict=True):
-            part = value[start : start + size].astype(jnp.bfloat16)
-            if other is None:
-                ref[:, at] = part
-            else:
-                second = value[other : other + size].astype(jnp.bfloat16)
-                ref[:, at] = jnp.where(flag_ref[0] == 1, part, second)
+        start = 0
+        for ref, size in zip(partial_refs, parts, strict=True):
+            ref[:, at] = value[start : start + size].astype(jnp.bfloat16)
+            start += size
 
     add_inputs(count - 1, write)
     value = scale_sum_ref[...]
@@ -311,7 +319,7 @@
 
 
 class Unit:
-    def __init__(self, order, lane, flag, pieces, parts, weights):
+    def __init__(self, order, lane, pieces, parts, weights):
         size = pieces[0].shape[0]
         rows = size * len(pieces)
         units, width = weights[0].shape
@@ -322,11 +330,11 @@
         bf16 = jnp.bfloat16
         out = order.call(
             functools.partial(unit_kernel, len(pieces), parts, count),
-            [lane, flag, *pieces, *weights],
-            [scalar, scalar] + [anywhere] * (len(pieces) + 3),
+            [lane, *pieces, *weights],
+            [scalar] + [anywhere] * (len(pieces) + 3),
             [jax.ShapeDtypeStruct((rows, units), bf16)] * 3
             + [jax.ShapeDtypeStruct((rows, width), bf16)]
-            + [jax.ShapeDtypeStruct((part[1], width + LANES), bf16) for part in parts],
+            + [jax.ShapeDtypeStruct((part, width + LANES), bf16) for part in parts],
             [anywhere] * 4 + [inside] * len(parts),
             scratch_shapes=[
                 pltpu.VMEM((rows, width), bf16),
@@ -348,10 +356,10 @@
         self.pieces = pieces
 
 
-def weight_kernel(n_right, n_left, *refs):
+def weight_kernel(n_right, n_left, n_out, *refs):
     right, refs = refs[:n_right], refs[n_right:]
-    left, refs = refs[:n_left], refs[n_left:]
-    out_ref, rows_ref, sems = refs
+    left, refs = refs[: n_left * n_out], refs[n_left * n_out :]
+    out_refs, (rows_ref, sems) = refs[:n_out], refs[n_out:]
     width = rows_ref.shape[1]
 
     @pl.when(pl.program_id(0) == 0)
@@ -370,30 +378,32 @@
         for copy in copies:
             copy.wait()
 
-    both = jnp.concatenate([ref[...] for ref in left], axis=0)
     tile = 1024
-    for start in range(0, width, tile):
-        at = slice(start, start + tile)
-        out_ref[:, at] = tn_dot(both, rows_ref[:, at]).astype(jnp.bfloat16)
-
-
-def weight_grad(order, right, left, width):
-    rows = sum(a.shape[0] for a in left)
+    for k, out_ref in enumerate(out_refs):
+        both = jnp.concatenate([ref[...] for ref in left[k * n_left : (k + 1) * n_left]], axis=0)
+        for start in range(0, width, tile):
+            at = slice(start, start + tile)
+            out_ref[:, at] = tn_dot(both, rows_ref[:, at]).astype(jnp.bfloat16)
+
+
+def weight_grads(order, right, lefts, width):
+    left = [a for one in lefts for a in one]
+    rows = sum(a.shape[0] for a in lefts[0])
     units = left[0].shape[1]
     anywhere = pl.BlockSpec(memory_space=pl.ANY)
     return order.call(
-        functools.partial(weight_kernel, len(right), len(left)),
+        functools.partial(weight_kernel, len(right), len(lefts[0]), len(lefts)),
         [*right, *left],
         [anywhere] * len(right)
         + [pl.BlockSpec((a.shape[0], F_BLOCK), lambda i: (0, i)) for a in left],
-        [jax.ShapeDtypeStruct((units, width), jnp.bfloat16)],
-        [pl.BlockSpec((F_BLOCK, width), lambda i: (i, 0))],
+        [jax.ShapeDtypeStruct((units, width), jnp.bfloat16)] * len(lefts),
+        [pl.BlockSpec((F_BLOCK, width), lambda i: (i, 0))] * len(lefts),
         grid=(units // F_BLOCK,),
         scratch_shapes=[
             pltpu.VMEM((rows, width), jnp.bfloat16),
             pltpu.SemaphoreType.DMA((len(right),)),
         ],
-    )[0]
+    )
 
 
 def unpack_kernel(slot_ref, *refs):
@@ -407,7 +417,8 @@
         placing = (at == slot).astype(jnp.float32).astype(jnp.bfloat16)
         total += jnp.dot(placing, ref[...], preferred_element_type=jnp.float32)
     grads_ref[...] = total[:, :width].astype(jnp.bfloat16)
-    scale_ref[...] = jnp.sum(total[:, width:], axis=1, keepdims=True)
+    ones = jnp.ones((8, LANES), jnp.bfloat16)
+    scale_ref[...] = nt_dot(ones, total[:, width:].astype(jnp.bfloat16))[0:1, :]
 
 
 def unpack(order, slot, groups, width):
@@ -419,7 +430,7 @@
         [inside] * (1 + len(groups)),
         [
             jax.ShapeDtypeStruct((rows, width), jnp.bfloat16),
-            jax.ShapeDtypeStruct((rows, 1), jnp.float32),
+            jax.ShapeDtypeStruct((1, rows), jnp.float32),
         ],
         [inside] * 2,
     )
@@ -434,14 +445,16 @@
     w_gate, w_up, w_down = gate_weight[0], up_weight[0], down_weight[0]
     lane = ((z * 2 + x) * 2).astype(jnp.int32).reshape(1)
 
-    route = routing[:, 0]
-    other = lax.bitwise_xor(route, e)
-    group = lax.bitwise_xor(other & 1, x) * 2 + (other >> 1)
-    index = jnp.arange(local_rows, dtype=jnp.int32)
-    earlier = (route[:, None] == route[None, :]) & (index[None, :] < index[:, None])
-    slot = group * size + jnp.sum(earlier.astype(jnp.int32), axis=1)
     scale_lanes = jnp.broadcast_to(gate_scale[:, None], (local_rows, LANES))
-    groups = pack(slot[None, :], token_rows, row_grads, scale_lanes, 4, size)
+    slot, *groups = pack(
+        e.astype(jnp.int32).reshape(1),
+        x.astype(jnp.int32).reshape(1),
+        routing,
+        token_rows,
+        row_grads,
+        scale_lanes,
+        size,
+    )
 
     def over_expert(a, g, cross=0):
         pairs = []
@@ -463,107 +476,75 @@
     flag = middle.astype(jnp.int32).reshape(1)
     weights = (w_gate, w_up, w_down)
     pair = 2 * size
-    x_near = along(near, OUTER)
+    near_1 = along(near, PAIRS[1])
     middle_near = along(near, MIDDLE)
-    xx_near = across(x_near)
-    second_near = along(x_near, MIDDLE)
+    order.wait(near_1, middle_near, near_other, far)
+    second_near = along(near_1, MIDDLE)
     out_near = along(middle_near, OUT)
+    swap_1 = across(near_1)
+    (near_2,) = choose(order, flag, [(second_near, out_near)])
     out_second = along(second_near, OUT)
-
-    y_near, far_1 = choose(order, flag, [(middle_near, out_near)], [far])
-    xy_near = across(y_near)
-    ends_far = along(far_1, ENDS)
-    in_far = along(far_1, IN_TWO)
+    swap_2 = across(near_2)
+    near_3, far_copy = choose(order, flag, [(middle_near, out_second)], [far], [swap_1, far_other])
+    swap_3 = across(near_3)
+    far_3 = along(far_copy, PAIRS[3])
+    far_1 = along(far_copy, PAIRS[1])
+    u0 = Unit(order, lane, [near, near_other, far, far_other], [pair, size, size], weights)
+    far_3, far_1, far_copy = choose(order, flag, [], [far_3, far_1, far], [swap_2])
+    far_swap_3 = across(far_3)
+    far_swap_1 = across(far_1)
+    far_2 = along(far_copy, PAIRS[2])
     u1 = Unit(
+        order, lane, [near_1, swap_1, near_2, swap_2, near_3, swap_3], [pair, pair, pair], weights
+    )
+    (far_2,) = choose(order, flag, [], [far_2], [far_swap_3])
+    far_swap_2 = across(far_2)
+    near_terms = [along(a, PAIRS[k + 1]) for k, a in enumerate(u1.partials)]
+    u2 = Unit(order, lane, [far_3, far_1, far_swap_3, far_swap_1], [pair, pair], weights)
+    others = across(u2.partials[1])
+    order.wait(near_terms[0], near_terms[2])
+    u3 = Unit(order, lane, [far_2, far_swap_2], [size, size], weights)
+    other_2 = across(u3.partials[1])
+    part_3, part_1 = sums(
+        order, [u2.partials[0], others], size, [[(0, 0), (1, 0)]], [[(0, size), (1, size)]]
+    )
+    far_terms = [along(part_3, PAIRS[3]), along(part_1, PAIRS[1])]
+    (part_2,) = sums(order, [u3.partials[0], other_2], size, [[(0, 0), (1, 0)]])
+    far_terms.append(along(part_2, PAIRS[2]))
+    terms = range(4)
+    near_own, rest = sums(
         order,
-        lane,
-        flag,
-        [near, near_other, far, far_other],
-        [(0, pair, None), (pair, size, None), (pair + size, size, None)],
-        weights,
-    )
-    z_near, far_2 = choose(order, flag, [(second_near, out_second)], [far])
-    xz_near = across(z_near)
-    middle_far = along(far_2, MIDDLE)
-    out_far = along(far_2, OUT_TWO)
-    x_far = along(far_2, OUTER)
-    z_far, w_other = choose(order, flag, [(in_far, ends_far)], [u1.partials[2]])
-    w_other = across(w_other)
-    xz_far = across(z_far)
-    u2 = Unit(
-        order,
-        lane,
-        flag,
-        [x_near, xx_near, y_near, xy_near, z_near, xz_near],
-        [(0, pair, None), (pair, pair, None), (2 * pair, pair, None), (2 * pair, pair, pair)],
-        weights,
-    )
-    y_far, x_far = choose(order, flag, [(middle_far, out_far)], [x_far], [xz_far, w_other])
-    xy_far = across(y_far)
-    xx_far = across(x_far)
-    x_part, y_part, z_part, s_part = u2.partials
-    near_terms = [
-        along(x_part, OUTER),
-        along(s_part, SKIP),
-        along(y_part, MIDDLE),
-        along(z_part, ENDS),
-    ]
-    u3 = Unit(
-        order,
-        lane,
-        flag,
-        [z_far, y_far, xz_far, xy_far],
-        [(0, pair, None), (pair, pair, None)],
-        weights,
-    )
-    zy_other = across(u3.partials[1])
-    u4 = Unit(
-        order, lane, flag, [x_far, xx_far], [(0, size, None), (size, size, None)], weights
-    )
-    x_other = across(u4.partials[1])
-    terms = range(2, 7)
-    z_part, y_part, s_part, near_own, near_other = sums(
-        order,
-        flag,
-        [u3.partials[0], zy_other, u1.partials[0], *near_terms],
-        [
-            (size, [(0, 0), (1, 0)], None),
-            (size, [(0, size), (1, size)], None),
-            (size, [(0, 0), (1, 0)], [(0, size), (1, size)]),
-            (size, [(k, 0) for k in terms], None),
-            (size, [(k, size) for k in terms], None),
-        ],
-    )
-    near_other = across(near_other)
-    far_terms = [along(s_part, SKIP), along(y_part, MIDDLE), along(z_part, ENDS)]
-
-    units_of = (u1, u2, u3, u4)
+        [u0.partials[0], *near_terms, u0.partials[2]],
+        size,
+        [[(k, 0) for k in terms]],
+        [[(k, size) for k in terms], [(4, 0)]],
+    )
+    rest = across(rest)
+
+    units_of = (u0, u1, u2, u3)
     rows = [piece for u in units_of for piece in u.pieces]
     scaled = [u.scaled for u in units_of]
     width = token_rows.shape[1]
 
-    def grad_of(right, name):
-        return weight_grad(order, right, [getattr(u, name) for u in units_of], width)
-
-    grad_down = grad_of(scaled, "hidden")
-    (x_part,) = sums(
-        order, flag, [u4.partials[0], x_other], [(size, [(0, 0), (1, 0)], None)]
-    )
-    far_terms.append(along(x_part, OUTER))
-    grad_gate = grad_of(rows, "gate_grad")
+    def grads_of(right, *names):
+        lefts = [[getattr(u, name) for u in units_of] for name in names]
+        return weight_grads(order, right, lefts, width)
+
+    grad_gate, grad_up = grads_of(rows, "gate_grad", "up_grad")
     near_own, far_own = sums(
         order,
-        flag,
-        [near_own, near_other, u1.partials[1], w_other, *far_terms],
-        [(size, [(0, 0), (1, 0)], None), (size, [(k, 0) for k in range(2, 8)], None)],
+        [near_own, rest, u0.partials[1], *far_terms],
+        size,
+        [[(0, 0), (1, 0)]],
+        [[(1, size), *[(k, 0) for k in range(2, 6)]]],
     )
     far_back = [over_expert(far_own, 1), over_expert(far_own, 1, 1)]
     near_back = [over_expert(near_own, 0), over_expert(near_own, 0, 1)]
-    grad_up = grad_of(rows, "up_grad")
+    (grad_down,) = grads_of(scaled, "hidden")
     input_grads, scale_grads = unpack(
-        order, slot[:, None], [near_back[0], far_back[0], near_back[1], far_back[1]], width
-    )
-    return (input_grads, scale_grads[:, 0], grad_gate[None], grad_up[None], grad_down[None])
+        order, slot.reshape(-1, 1), [near_back[0], far_back[0], near_back[1], far_back[1]], width
+    )
+    return (input_grads, scale_grads[0], grad_gate[None], grad_up[None], grad_down[None])
 
 
 def plain_device(token_rows, row_grads, gate_scale, routing, gate_weight, up_weight, down_weight):

time: 494 us -> 309 us (0.63)
  Pallas kernels: 370 us -> 193 us
  starting transfers between devices: 58.5 us -> 49.9 us
    pallas_call x15 -> x17, Pallas kernels: 369 us -> 188 us  [call(): pl.pallas_call(body, in_specs=[*in_specs, anywhere], out_specs=[*out_spec...]
    ppermute x18 -> x14, waiting for transfers between devices: 20.5 us -> 44.4 us  [along(): return lax.ppermute(a, 'dp', pairs)]
    ppermute x8, waiting for transfers between devices: 14.6 us -> 0.08 us  [over_expert(): return lax.ppermute(a, ('expert', 'etensor'), pairs)]
    ppermute x18 -> x14, starting transfers between devices: 34 us -> 20 us  [along(): return lax.ppermute(a, 'dp', pairs)]
    ppermute x10 -> x9, waiting for transfers between devices: 12.9 us -> 4.81 us  [across(): return lax.ppermute(a, 'etensor', ((0, 1), (1, 0)))]
    ppermute x10 -> x9, starting transfers between devices: 14.2 us -> 18.6 us  [across(): return lax.ppermute(a, 'etensor', ((0, 1), (1, 0)))]
    unnamed x65 -> x57, local copies, waits for them, and re-layouts: 10.6 us -> 12.3 us
  transfers between devices with their start and end apart: 36 -> 31, of which waited for: 5 -> 7; matrix products, arithmetic and copies ran while one was open for 0% -> 0% of each run, Pallas kernels for 63% -> 58%
where the time goes in v2:
time: 309 us; the launch traced here: 308 us
  Pallas kernels  193 us (62%)
  starting transfers between devices  49.9 us (16%)
  waiting for transfers between devices  49.3 us (16%)
  local copies, waits for them, and re-layouts  15 us (5%)
    pallas_call x17, Pallas kernels, call(): pl.pallas_call(body, in_specs=[*in_specs, anywhere], out_specs=[*out_spec...  188 us
    ppermute x14, waiting for transfers between devices, along(): return lax.ppermute(a, 'dp', pairs)  44.4 us
    ppermute x14, starting transfers between devices, along(): return lax.ppermute(a, 'dp', pairs)  20 us
    ppermute x9, starting transfers between devices, across(): return lax.ppermute(a, 'etensor', ((0, 1), (1, 0)))  18.6 us
    unnamed x57, local copies, waits for them, and re-layouts  12.3 us
    ppermute x8, starting transfers between devices, over_expert(): return lax.ppermute(a, ('expert', 'etensor'), pairs)  11.3 us
  transfers between devices with their start and end apart: 31, of which 7 were waited for; matrix products, arithmetic and copies ran while one was open for 0% of the time, Pallas kernels for 58%

profile of v2, /device:TPU:0, one launch (start us, length us, event | category | flops | bytes accessed | tf_op | source)
XLA Modules:
  0.0 307.8 jit_solution(16921079013691109289)
XLA Ops:
  0.6 1.4 copy.29.down_ref
  2.0 1.3 broadcast_in_dim.18.scale_ref
  3.4 4.6 %shard_map.110 = (s32[1,128]{1,0:T(1,128)}, bf16[48,8320]{1,0:T(8,128)(2,1)}, bf16[48,8320]{1,0:T(8,128)(2,1)}, bf16[48,8320]{1,0:T(8,128)(2,1)}, bf16[48,8320]{1,0:T(8,128)(2,1)}) custom-call(s32[1]{0:T(128)} %bitcast.e_ref, s32[1]{0:T(128)} %bitcast.1.x_ref, s32[1,128]{1,0:T(1,128)} %bitcast.25, s32[128,1]{1,0:T(8,128)} %copy.29.down_ref, ...), custom_call_target="tpu_custom_call" | custom-call | tf_op jit(solution)/shard_map/pallas_call | solution.py:66
  7.9 1.8 collective-permute-start
  9.7 3.0 collective-permute-start.5
  12.8 1.6 collective-permute-start.4
  14.4 1.5 collective-permute-start.2
  15.9 14.7 %collective-permute-done.5.refs_0_.refs_1_.refs_4_ = bf16[48,8320]{1,0:T(8,128)(2,1)S(1)} collective-permute-done((bf16[48,8320]{1,0:T(8,128)(2,1)S(1)}, bf16[48,8320]{1,0:T(8,128)(2,1)S(1)}, u32[]{:S(2)}, u32[]{:S(2)}) %collective-permute-start.5) | collective-permute-done | bytes 798752 | tf_op jit(solution)/shard_map/ppermute | solution.py:468
  30.6 1.6 collective-permute-start.6
  32.1 1.9 collective-permute-start.1
  34.0 1.3 collective-permute-start.9
  35.3 1.9 collective-permute-start.3
  37.2 4.1 %collective-permute-start.8 = (bf16[48,8320]{1,0:T(8,128)(2,1)S(1)}, bf16[48,8320]{1,0:T(8,128)(2,1)}, u32[]{:S(2)}, u32[]{:S(2)}) collective-permute-start(bf16[48,8320]{1,0:T(8,128)(2,1)S(1)} %collective-permute-done.5.refs_0_.refs_1_.refs_4_), channel_id=1, source_target_pairs={{0,1},{1,0},{2,3},{3,2},{4,5},{5,4},{6,7},{7,6},{8,9},{9,8},{10,11... | collective-permute-start | bytes 2396168 | tf_op jit(solution)/shard_map/ppermute | solution.py:471
  41.4 1.3 collective-permute-start.7
  42.7 0.6 broadcast_in_dim.19.refs_4_
  43.6 14.4 %collective-permute-done.9.refs_2_ = bf16[48,8320]{1,0:T(8,128)(2,1)} collective-permute-done((bf16[48,8320]{1,0:T(8,128)(2,1)}, bf16[48,8320]{1,0:T(8,128)(2,1)}, u32[]{:S(2)}, u32[]{:S(2)}) %collective-permute-start.9) | collective-permute-done | bytes 798752 | tf_op jit(solution)/shard_map/ppermute | solution.py:468
  58.0 2.3 shard_map.112
  60.3 4.3 %collective-permute-start.10 = (bf16[48,8320]{1,0:T(8,128)(2,1)}, bf16[48,8320]{1,0:T(8,128)(2,1)S(1)}, u32[]{:S(2)}, u32[]{:S(2)}) collective-permute-start(bf16[48,8320]{1,0:T(8,128)(2,1)} %get-tuple-element.77.refs_3_.refs_6_), channel_id=1, source_target_pairs={{0,1},{1,0},{2,3},{3,2},{4,5},{5,4},{6,7},{7,6},{8,9},{9,8},{10,11... | collective-permute-start | bytes 2396168 | tf_op jit(solution)/shard_map/ppermute | solution.py:471
  64.6 10.3 %collective-permute-done.7.refs_2_ = bf16[48,8320]{1,0:T(8,128)(2,1)} collective-permute-done((bf16[48,8320]{1,0:T(8,128)(2,1)}, bf16[48,8320]{1,0:T(8,128)(2,1)}, u32[]{:S(2)}, u32[]{:S(2)}) %collective-permute-start.7) | collective-permute-done | bytes 798752 | tf_op jit(solution)/shard_map/ppermute | solution.py:468
  74.9 2.8 shard_map.113
  77.7 2.4 collective-permute-start.12
  80.2 3.1 collective-permute-start.11
  83.2 28.7 %shard_map.114 = (bf16[192,1792]{1,0:T(8,128)(2,1)}, bf16[192,1792]{1,0:T(8,128)(2,1)}, bf16[192,1792]{1,0:T(8,128)(2,1)}, bf16[192,4096]{1,0:T(8,128)(2,1)}, bf...) custom-call(s32[1]{0:T(128)} %bitcast.4.refs_0_, ...), custom_call_target="tpu_custom_call", output_to_operand_aliasing={{7}: (8, {})} | custom-call | tf_op jit(solution)/shard_map/pallas_call | solution.py:99
  112.0 4.6 %collective-permute-done.13.refs_2_ = bf16[48,8320]{1,0:T(8,128)(2,1)S(1)} collective-permute-done((bf16[48,8320]{1,0:T(8,128)(2,1)}, bf16[48,8320]{1,0:T(8,128)(2,1)S(1)}, u32[]{:S(2)}, u32[]{:S(2)}) %collective-permute-start.13) | collective-permute-done | bytes 798752 | tf_op jit(solution)/shard_map/ppermute | solution.py:468
  116.6 0.9 copy-done.17
  117.5 3.2 %shard_map.115 = (bf16[48,8320]{1,0:T(8,128)(2,1)}, bf16[48,8320]{1,0:T(8,128)(2,1)}, bf16[48,8320]{1,0:T(8,128)(2,1)}, f32[8,128]{1,0:T(8,128)}) custom-call(s32[1]{0:T(128)} %bitcast.8.refs_0_, bf16[48,8320]{1,0:T(8,128)(2,1)} %copy-done.15, bf16[48,8320]{1,0:T(8,128)(2,1)} %copy-done.17, ...), custom_call_target="tpu_custom_call", output_to_operand_aliasing={{3}: (5, {})} | custom-call | tf_op jit(solution)/shard_map/pallas_call | solution.py:99
  120.6 0.6 collective-permute-start.17
  121.2 1.5 collective-permute-start.18
  122.6 0.6 collective-permute-start.20
  123.2 0.9 copy-done.10
  124.1 32.5 %shard_map.116 = (bf16[288,1792]{1,0:T(8,128)(2,1)}, bf16[288,1792]{1,0:T(8,128)(2,1)}, bf16[288,1792]{1,0:T(8,128)(2,1)}, bf16[288,4096]{1,0:T(8,128)(2,1)}, bf...) custom-call(s32[1]{0:T(128)} %bitcast.4.refs_0_, ...), custom_call_target="tpu_custom_call", output_to_operand_aliasing={{7}: (10, {})} | custom-call | tf_op jit(solution)/shard_map/pallas_call | solution.py:99
  156.6 1.7 collective-permute-start.14
  158.3 2.2 collective-permute-start.16
  160.5 0.9 copy-done.16
  161.7 2.1 shard_map.117
  163.8 1.5 collective-permute-start.19
  165.2 0.9 copy-done.11
  166.2 28.4 %shard_map.118 = (bf16[192,1792]{1,0:T(8,128)(2,1)}, bf16[192,1792]{1,0:T(8,128)(2,1)}, bf16[192,1792]{1,0:T(8,128)(2,1)}, bf16[192,4096]{1,0:T(8,128)(2,1)}, bf...) custom-call(s32[1]{0:T(128)} %bitcast.4.refs_0_, ...), custom_call_target="tpu_custom_call", output_to_operand_aliasing={{6}: (8, {})} | custom-call | tf_op jit(solution)/shard_map/pallas_call | solution.py:99
  194.6 0.6 collective-permute-start.22
  195.3 0.9 copy-done.6
  196.5 0.9 copy-done.8
  197.4 25.5 %shard_map.120 = (bf16[96,1792]{1,0:T(8,128)(2,1)}, bf16[96,1792]{1,0:T(8,128)(2,1)}, bf16[96,1792]{1,0:T(8,128)(2,1)}, bf16[96,4096]{1,0:T(8,128)(2,1)}, bf16[4...) custom-call(s32[1]{0:T(128)} %bitcast.4.refs_0_, ...), custom_call_target="tpu_custom_call", output_to_operand_aliasing={{6}: (6, {})} | custom-call | tf_op jit(solution)/shard_map/pallas_call | solution.py:99
  222.9 1.5 collective-permute-start.21
  224.4 0.9 copy-done.14
  225.3 2.4 shard_map.121
  227.7 4.8 %collective-permute-done.21.refs_1_ = bf16[48,4224]{1,0:T(8,128)(2,1)S(1)} collective-permute-done((bf16[48,4224]{1,0:T(8,128)(2,1)}, bf16[48,4224]{1,0:T(8,128)(2,1)S(1)}, u32[]{:S(2)}, u32[]{:S(2)}) %collective-permute-start.21) | collective-permute-done | bytes 405536 | tf_op jit(solution)/shard_map/ppermute | solution.py:471
  232.5 0.7 copy-done.22
  233.3 2.0 shard_map.122
  235.3 0.9 copy-done.12
  236.1 3.3 %shard_map.123 = (bf16[48,4224]{1,0:T(8,128)(2,1)}, bf16[96,4224]{1,0:T(8,128)(2,1)}, f32[8,128]{1,0:T(8,128)}) custom-call(bf16[96,4224]{1,0:T(8,128)(2,1)} %get-tuple-element.76.refs_0_, bf16[96,4224]{1,0:T(8,128)(2,1)} %copy-done.6, bf16[96,4224]{1,0:T(8,128)(2,1)} %copy-done.12, bf16[96,4224]{1,0:T(8,128)(2,1)} %copy-done.7, ...), custom_call_target="tpu_custom_call", output_to_operand_aliasing={{2}: (5, {})} | custom-call | tf_op jit(solution)/shard_map/pallas_call | solution.py:99
  239.5 1.5 collective-permute-start.23
  240.9 1.5 collective-permute-start.24
  242.5 1.7 collective-permute-start.25
  244.1 1.2 collective-permute-start.26
  245.3 30.2 %shard_map.124 = (bf16[1792,4096]{1,0:T(8,128)(2,1)}, bf16[1792,4096]{1,0:T(8,128)(2,1)}, f32[8,128]{1,0:T(8,128)}) custom-call(bf16[48,8320]{1,0:T(8,128)(2,1)} %copy-done.9, bf16[48,8320]{1,0:T(8,128)(2,1)} %copy-done.2, bf16[48,8320]{1,0:T(8,128)(2,1)} %copy-done, bf16[48,8320]{1,0:T(8,128)(2,1)} %copy-done.3, ...), custom_call_target="tpu_custom_call", output_to_operand_aliasing={{2}: (24, {})} | custom-call | tf_op jit(solution)/shard_map/pallas_call | solution.py:99
  275.6 0.4 collective-permute-done.26.refs_5_
  277.0 2.8 shard_map.125
  279.8 1.6 collective-permute-start.27
  281.5 1.5 collective-permute-start.28
  283.0 1.0 collective-permute-start.29
  284.0 0.7 copy.30.refs_0_
  284.7 18.2 %shard_map.126 = (bf16[1792,4096]{1,0:T(8,128)(2,1)}, f32[8,128]{1,0:T(8,128)}) custom-call(bf16[192,4096]{1,0:T(8,128)(2,1)} %get-tuple-element.118.refs_0_, bf16[288,4096]{1,0:T(8,128)(2,1)} %get-tuple-element.119.refs_1_, bf16[192,4096]{1,0:T(8,128)(2,1)} %get-tuple-element.120.refs_2_, ...), custom_call_target="tpu_custom_call", output_to_operand_aliasing={{1}: (8, {})} | custom-call | tf_op jit(solution)/shard_map/pallas_call | solution.py:99
  303.1 0.7 copy-done.18
  304.2 3.7 %shard_map.127 = (bf16[128,4096]{1,0:T(8,128)(2,1)}, f32[1,128]{1,0:T(1,128)}, f32[8,128]{1,0:T(8,128)}) custom-call(s32[128,1]{1,0:T(8,128)} %copy.30.refs_0_, bf16[48,4224]{1,0:T(8,128)(2,1)} %copy-done.18, bf16[48,4224]{1,0:T(8,128)(2,1)} %copy-done.19, bf16[48,4224]{1,0:T(8,128)(2,1)} %copy-done.20, ...), custom_call_target="tpu_custom_call", output_to_operand_aliasing={{2}: (5, {})} | custom-call | tf_op jit(solution)/shard_map/pallas_call | solution.py:99
  (76 shorter events, 2.5 us)
Async XLA Ops:
  7.9 1.8 collective-permute-start
  9.7 31.6 %copy-start.9 = (bf16[48,8320]{1,0:T(8,128)(2,1)}, bf16[48,8320]{1,0:T(8,128)(2,1)S(1)}, u32[]{:S(2)}) copy-start(bf16[48,8320]{1,0:T(8,128)(2,1)S(1)} %collective-permute-done.refs_1_.refs_0_) | copy-start | bytes 2396164
  9.7 20.8 %collective-permute-start.5 = (bf16[48,8320]{1,0:T(8,128)(2,1)S(1)}, bf16[48,8320]{1,0:T(8,128)(2,1)S(1)}, u32[]{:S(2)}, u32[]{:S(2)}) collective-permute-start(bf16[48,8320]{1,0:T(8,128)(2,1)S(1)} %collective-permute-done.refs_1_.refs_0_), channel_id=1, source_target_pairs={{0,8},{8,0},{16,24},{24,16},{1,9},{9,1},{17,25},{25,17},{2,10},{10... | collective-permute-start | bytes 2396168 | tf_op jit(solution)/shard_map/ppermute | solution.py:468
  12.8 21.3 %collective-permute-start.4 = (bf16[48,8320]{1,0:T(8,128)(2,1)S(1)}, bf16[48,8320]{1,0:T(8,128)(2,1)}, u32[]{:S(2)}, u32[]{:S(2)}) collective-permute-start(bf16[48,8320]{1,0:T(8,128)(2,1)S(1)} %collective-permute-done.refs_1_.refs_0_), channel_id=1, source_target_pairs={{8,16},{16,8},{9,17},{17,9},{10,18},{18,10},{11,19},{19,11},{12,20... | collective-permute-start | bytes 2396168 | tf_op jit(solution)/shard_map/ppermute | solution.py:468
  14.4 22.8 %collective-permute-start.2 = (bf16[48,8320]{1,0:T(8,128)(2,1)}, bf16[48,8320]{1,0:T(8,128)(2,1)S(1)}, u32[]{:S(2)}, u32[]{:S(2)}) collective-permute-start(bf16[48,8320]{1,0:T(8,128)(2,1)} %get-tuple-element.72), channel_id=1, source_target_pairs={{0,4},{1,7},{2,6},{3,5},{4,0},{5,3},{6,2},{7,1},{8,12},{9,15},{10,... | collective-permute-start | bytes 2396168 | tf_op jit(solution)/shard_map/ppermute | solution.py:465
  30.6 12.8 %copy-start.1 = (bf16[48,8320]{1,0:T(8,128)(2,1)}, bf16[48,8320]{1,0:T(8,128)(2,1)S(1)}, u32[]{:S(2)}) copy-start(bf16[48,8320]{1,0:T(8,128)(2,1)S(1)} %collective-permute-done.5.refs_0_.refs_1_.refs_4_) | copy-start | bytes 2396164
  30.6 10.8 %collective-permute-start.6 = (bf16[48,8320]{1,0:T(8,128)(2,1)S(1)}, bf16[48,8320]{1,0:T(8,128)(2,1)}, u32[]{:S(2)}, u32[]{:S(2)}) collective-permute-start(bf16[48,8320]{1,0:T(8,128)(2,1)S(1)} %collective-permute-done.5.refs_0_.refs_1_.refs_4_), channel_id=1, source_target_pairs={{8,16},{16,8},{9,17},{17,9},{10,18},{18,10},{11,19},{19,11},{12,20... | collective-permute-start | bytes 2396168 | tf_op jit(solution)/shard_map/ppermute | solution.py:468
  32.1 10.5 %collective-permute-start.1 = (bf16[48,8320]{1,0:T(8,128)(2,1)}, bf16[48,8320]{1,0:T(8,128)(2,1)S(1)}, u32[]{:S(2)}, u32[]{:S(2)}) collective-permute-start(bf16[48,8320]{1,0:T(8,128)(2,1)} %get-tuple-element.71), channel_id=1, source_target_pairs={{0,2},{1,1},{2,0},{3,3},{4,6},{5,5},{6,4},{7,7},{8,10},{9,9},{10,8... | collective-permute-start | bytes 2396168 | tf_op jit(solution)/shard_map/ppermute | solution.py:465
  34.0 23.9 %collective-permute-start.9 = (bf16[48,8320]{1,0:T(8,128)(2,1)}, bf16[48,8320]{1,0:T(8,128)(2,1)}, u32[]{:S(2)}, u32[]{:S(2)}) collective-permute-start(bf16[48,8320]{1,0:T(8,128)(2,1)} %collective-permute-done.4.refs_1_), channel_id=1, source_target_pairs={{8,0},{16,24},{9,1},{17,25},{10,2},{18,26},{11,3},{19,27},{12,4},{... | collective-permute-start | bytes 2396168 | tf_op jit(solution)/shard_map/ppermute | solution.py:468
  35.3 29.3 %collective-permute-start.3 = (bf16[48,8320]{1,0:T(8,128)(2,1)}, bf16[48,8320]{1,0:T(8,128)(2,1)S(1)}, u32[]{:S(2)}, u32[]{:S(2)}) collective-permute-start(bf16[48,8320]{1,0:T(8,128)(2,1)} %get-tuple-element.73), channel_id=1, source_target_pairs={{0,6},{1,5},{2,4},{3,7},{4,2},{5,1},{6,0},{7,3},{8,14},{9,13},{10,... | collective-permute-start | bytes 2396168 | tf_op jit(solution)/shard_map/ppermute | solution.py:465
  37.2 6.1 %copy-start = (bf16[48,8320]{1,0:T(8,128)(2,1)}, bf16[48,8320]{1,0:T(8,128)(2,1)S(1)}, u32[]{:S(2)}) copy-start(bf16[48,8320]{1,0:T(8,128)(2,1)S(1)} %collective-permute-done.2.refs_3_.refs_2_) | copy-start | bytes 2396164
  37.2 27.4 %collective-permute-start.8 = (bf16[48,8320]{1,0:T(8,128)(2,1)S(1)}, bf16[48,8320]{1,0:T(8,128)(2,1)}, u32[]{:S(2)}, u32[]{:S(2)}) collective-permute-start(bf16[48,8320]{1,0:T(8,128)(2,1)S(1)} %collective-permute-done.5.refs_0_.refs_1_.refs_4_), channel_id=1, source_target_pairs={{0,1},{1,0},{2,3},{3,2},{4,5},{5,4},{6,7},{7,6},{8,9},{9,8},{10,11... | collective-permute-start | bytes 2396168 | tf_op jit(solution)/shard_map/ppermute | solution.py:471
  41.4 33.5 %collective-permute-start.7 = (bf16[48,8320]{1,0:T(8,128)(2,1)}, bf16[48,8320]{1,0:T(8,128)(2,1)}, u32[]{:S(2)}, u32[]{:S(2)}) collective-permute-start(bf16[48,8320]{1,0:T(8,128)(2,1)} %collective-permute-done.6.refs_1_), channel_id=1, source_target_pairs={{8,0},{16,24},{9,1},{17,25},{10,2},{18,26},{11,3},{19,27},{12,4},{... | collective-permute-start | bytes 2396168 | tf_op jit(solution)/shard_map/ppermute | solution.py:468
  42.7 0.9 copy-start.2
  60.3 51.6 %collective-permute-start.10 = (bf16[48,8320]{1,0:T(8,128)(2,1)}, bf16[48,8320]{1,0:T(8,128)(2,1)S(1)}, u32[]{:S(2)}, u32[]{:S(2)}) collective-permute-start(bf16[48,8320]{1,0:T(8,128)(2,1)} %get-tuple-element.77.refs_3_.refs_6_), channel_id=1, source_target_pairs={{0,1},{1,0},{2,3},{3,2},{4,5},{5,4},{6,7},{7,6},{8,9},{9,8},{10,11... | collective-permute-start | bytes 2396168 | tf_op jit(solution)/shard_map/ppermute | solution.py:471
  64.6 10.3 %copy-start.3 = (bf16[48,8320]{1,0:T(8,128)(2,1)}, bf16[48,8320]{1,0:T(8,128)(2,1)S(1)}, u32[]{:S(2)}) copy-start(bf16[48,8320]{1,0:T(8,128)(2,1)S(1)} %collective-permute-done.3.refs_5_.refs_4_.refs_3_) | copy-start | bytes 2396164
  77.7 34.2 %collective-permute-start.12 = (bf16[48,8320]{1,0:T(8,128)(2,1)}, bf16[48,8320]{1,0:T(8,128)(2,1)S(1)}, u32[]{:S(2)}, u32[]{:S(2)}) collective-permute-start(bf16[48,8320]{1,0:T(8,128)(2,1)} %get-tuple-element.79), channel_id=1, source_target_pairs={{0,24},{8,16},{16,8},{24,0},{1,25},{9,17},{17,9},{25,1},{2,26},{10... | collective-permute-start | bytes 2396168 | tf_op jit(solution)/shard_map/ppermute | solution.py:468
  80.2 36.4 %collective-permute-start.13 = (bf16[48,8320]{1,0:T(8,128)(2,1)}, bf16[48,8320]{1,0:T(8,128)(2,1)S(1)}, u32[]{:S(2)}, u32[]{:S(2)}) collective-permute-start(bf16[48,8320]{1,0:T(8,128)(2,1)} %get-tuple-element.79), channel_id=1, source_target_pairs={{0,8},{8,0},{16,24},{24,16},{1,9},{9,1},{17,25},{25,17},{2,10},{10... | collective-permute-start | bytes 2396168 | tf_op jit(solution)/shard_map/ppermute | solution.py:468
  80.2 43.0 %collective-permute-start.11 = (bf16[48,8320]{1,0:T(8,128)(2,1)}, bf16[48,8320]{1,0:T(8,128)(2,1)S(1)}, u32[]{:S(2)}, u32[]{:S(2)}) collective-permute-start(bf16[48,8320]{1,0:T(8,128)(2,1)} %get-tuple-element.78.refs_5_.refs_8_), channel_id=1, source_target_pairs={{0,1},{1,0},{2,3},{3,2},{4,5},{5,4},{6,7},{7,6},{8,9},{9,8},{10,11... | collective-permute-start | bytes 2396168 | tf_op jit(solution)/shard_map/ppermute | solution.py:471
  111.9 4.6 %copy-start.4 = (bf16[48,8320]{1,0:T(8,128)(2,1)}, bf16[48,8320]{1,0:T(8,128)(2,1)S(1)}, u32[]{:S(2)}) copy-start(bf16[48,8320]{1,0:T(8,128)(2,1)S(1)} %collective-permute-done.10.refs_4_.refs_7_) | copy-start | bytes 2396164
  112.0 4.6 %copy-start.15 = (bf16[48,8320]{1,0:T(8,128)(2,1)}, bf16[48,8320]{1,0:T(8,128)(2,1)S(1)}, u32[]{:S(2)}) copy-start(bf16[48,8320]{1,0:T(8,128)(2,1)S(1)} %collective-permute-done.12.refs_1_) | copy-start | bytes 2396164
  116.6 0.9 copy-start.17
  120.6 39.9 %collective-permute-start.17 = (bf16[48,8320]{1,0:T(8,128)(2,1)}, bf16[48,8320]{1,0:T(8,128)(2,1)S(1)}, u32[]{:S(2)}, u32[]{:S(2)}) collective-permute-start(bf16[48,8320]{1,0:T(8,128)(2,1)} %get-tuple-element.86), channel_id=1, source_target_pairs={{0,16},{8,24},{16,0},{24,8},{1,17},{9,25},{17,1},{25,9},{2,18},{10... | collective-permute-start | bytes 2396168 | tf_op jit(solution)/shard_map/ppermute | solution.py:468
  121.2 39.3 %collective-permute-start.18 = (bf16[48,8320]{1,0:T(8,128)(2,1)}, bf16[48,8320]{1,0:T(8,128)(2,1)S(1)}, u32[]{:S(2)}, u32[]{:S(2)}) collective-permute-start(bf16[48,8320]{1,0:T(8,128)(2,1)} %get-tuple-element.87.refs_1_.refs_10_), channel_id=1, source_target_pairs={{0,1},{1,0},{2,3},{3,2},{4,5},{5,4},{6,7},{7,6},{8,9},{9,8},{10,11... | collective-permute-start | bytes 2396168 | tf_op jit(solution)/shard_map/ppermute | solution.py:471
  122.6 42.6 %collective-permute-start.20 = (bf16[48,8320]{1,0:T(8,128)(2,1)}, bf16[48,8320]{1,0:T(8,128)(2,1)S(1)}, u32[]{:S(2)}, u32[]{:S(2)}) collective-permute-start(bf16[48,8320]{1,0:T(8,128)(2,1)} %get-tuple-element.90.refs_2_.refs_11_), channel_id=1, source_target_pairs={{0,1},{1,0},{2,3},{3,2},{4,5},{5,4},{6,7},{7,6},{8,9},{9,8},{10,11... | collective-permute-start | bytes 2396168 | tf_op jit(solution)/shard_map/ppermute | solution.py:471
  123.2 0.9 copy-start.10
  156.6 38.6 %collective-permute-start.14 = (bf16[96,4224]{1,0:T(8,128)(2,1)}, bf16[96,4224]{1,0:T(8,128)(2,1)S(1)}, u32[]{:S(2)}, u32[]{:S(2)}) collective-permute-start(bf16[96,4224]{1,0:T(8,128)(2,1)} %get-tuple-element.82), channel_id=1, source_target_pairs={{0,8},{8,0},{16,24},{24,16},{1,9},{9,1},{17,25},{25,17},{2,10},{10... | collective-permute-start | bytes 2433032 | tf_op jit(solution)/shard_map/ppermute | solution.py:468
  158.3 36.9 %collective-permute-start.16 = (bf16[96,4224]{1,0:T(8,128)(2,1)}, bf16[96,4224]{1,0:T(8,128)(2,1)S(1)}, u32[]{:S(2)}, u32[]{:S(2)}) collective-permute-start(bf16[96,4224]{1,0:T(8,128)(2,1)} %get-tuple-element.84), channel_id=1, source_target_pairs={{0,24},{8,16},{16,8},{24,0},{1,25},{9,17},{17,9},{25,1},{2,26},{10... | collective-permute-start | bytes 2433032 | tf_op jit(solution)/shard_map/ppermute | solution.py:468
  160.5 0.9 copy-start.16
  160.5 1.2 copy-start.5
  163.8 32.7 %collective-permute-start.19 = (bf16[48,8320]{1,0:T(8,128)(2,1)}, bf16[48,8320]{1,0:T(8,128)(2,1)S(1)}, u32[]{:S(2)}, u32[]{:S(2)}) collective-permute-start(bf16[48,8320]{1,0:T(8,128)(2,1)} %get-tuple-element.89.refs_1_.refs_14_), channel_id=1, source_target_pairs={{0,1},{1,0},{2,3},{3,2},{4,5},{5,4},{6,7},{7,6},{8,9},{9,8},{10,11... | collective-permute-start | bytes 2396168 | tf_op jit(solution)/shard_map/ppermute | solution.py:471
  165.2 0.9 copy-start.11
  166.2 29.1 %copy-start.27 = (bf16[96,4224]{1,0:T(8,128)(2,1)S(1)}, bf16[96,4224]{1,0:T(8,128)(2,1)}, u32[]{:S(2)}) copy-start(bf16[96,4224]{1,0:T(8,128)(2,1)} %get-tuple-element.83) | copy-start | bytes 2433028
  194.6 29.8 %collective-permute-start.22 = (bf16[96,4224]{1,0:T(8,128)(2,1)}, bf16[96,4224]{1,0:T(8,128)(2,1)S(1)}, u32[]{:S(2)}, u32[]{:S(2)}) collective-permute-start(bf16[96,4224]{1,0:T(8,128)(2,1)} %get-tuple-element.96), channel_id=1, source_target_pairs={{0,1},{1,0},{2,3},{3,2},{4,5},{5,4},{6,7},{7,6},{8,9},{9,8},{10,11... | collective-permute-start | bytes 2433032 | tf_op jit(solution)/shard_map/ppermute | solution.py:471
  195.2 40.0 %collective-permute-start.15 = (bf16[96,4224]{1,0:T(8,128)(2,1)S(1)}, bf16[96,4224]{1,0:T(8,128)(2,1)S(1)}, u32[]{:S(2)}, u32[]{:S(2)}) collective-permute-start(bf16[96,4224]{1,0:T(8,128)(2,1)S(1)} %copy-done.27), channel_id=1, source_target_pairs={{0,16},{8,24},{16,0},{24,8},{1,17},{9,25},{17,1},{25,9},{2,18},{10... | collective-permute-start | bytes 2433032 | tf_op jit(solution)/shard_map/ppermute | solution.py:468
  195.3 0.9 copy-start.6
  195.3 1.2 copy-start.7
  196.5 0.9 copy-start.8
  222.9 61.1 %copy-start.26 = (s32[1,128]{1,0:T(1,128)S(1)}, s32[1,128]{1,0:T(1,128)}, u32[]{:S(2)}) copy-start(s32[1,128]{1,0:T(1,128)} %get-tuple-element.69) | copy-start | bytes 1540
  222.9 9.6 %collective-permute-start.21 = (bf16[48,4224]{1,0:T(8,128)(2,1)}, bf16[48,4224]{1,0:T(8,128)(2,1)S(1)}, u32[]{:S(2)}, u32[]{:S(2)}) collective-permute-start(bf16[48,4224]{1,0:T(8,128)(2,1)} %get-tuple-element.94), channel_id=1, source_target_pairs={{0,1},{1,0},{2,3},{3,2},{4,5},{5,4},{6,7},{7,6},{8,9},{9,8},{10,11... | collective-permute-start | bytes 1216520 | tf_op jit(solution)/shard_map/ppermute | solution.py:471
  224.4 0.9 copy-start.14
  232.5 0.8 copy-start.22
  235.2 0.9 copy-start.12
  239.5 36.5 %collective-permute-start.23 = (bf16[96,4224]{1,0:T(8,128)(2,1)}, bf16[96,4224]{1,0:T(8,128)(2,1)S(1)}, u32[]{:S(2)}, u32[]{:S(2)}) collective-permute-start(bf16[96,4224]{1,0:T(8,128)(2,1)} %get-tuple-element.101), channel_id=1, source_target_pairs={{0,1},{1,0},{2,3},{3,2},{4,5},{5,4},{6,7},{7,6},{8,9},{9,8},{10,11... | collective-permute-start | bytes 2433032 | tf_op jit(solution)/shard_map/ppermute | solution.py:471
  240.9 34.6 %collective-permute-start.24 = (bf16[48,4224]{1,0:T(8,128)(2,1)}, bf16[48,4224]{1,0:T(8,128)(2,1)S(1)}, u32[]{:S(2)}, u32[]{:S(2)}) collective-permute-start(bf16[48,4224]{1,0:T(8,128)(2,1)} %get-tuple-element.103), channel_id=1, source_target_pairs={{0,24},{8,16},{16,8},{24,0},{1,25},{9,17},{17,9},{25,1},{2,26},{10... | collective-permute-start | bytes 1216520 | tf_op jit(solution)/shard_map/ppermute | solution.py:468
  242.5 33.1 %collective-permute-start.25 = (bf16[48,4224]{1,0:T(8,128)(2,1)}, bf16[48,4224]{1,0:T(8,128)(2,1)S(1)}, u32[]{:S(2)}, u32[]{:S(2)}) collective-permute-start(bf16[48,4224]{1,0:T(8,128)(2,1)} %get-tuple-element.104), channel_id=1, source_target_pairs={{0,8},{8,0},{16,24},{24,16},{1,9},{9,1},{17,25},{25,17},{2,10},{10... | collective-permute-start | bytes 1216520 | tf_op jit(solution)/shard_map/ppermute | solution.py:468
  244.1 31.8 %collective-permute-start.26 = (bf16[48,4224]{1,0:T(8,128)(2,1)}, bf16[48,4224]{1,0:T(8,128)(2,1)S(1)}, u32[]{:S(2)}, u32[]{:S(2)}) collective-permute-start(bf16[48,4224]{1,0:T(8,128)(2,1)} %get-tuple-element.105), channel_id=1, source_target_pairs={{0,16},{8,24},{16,0},{24,8},{1,17},{9,25},{17,1},{25,9},{2,18},{10... | collective-permute-start | bytes 1216520 | tf_op jit(solution)/shard_map/ppermute | solution.py:468
  275.5 0.8 copy-start.23
  275.5 0.9 copy-start.24
  276.0 0.8 copy-start.25
  276.0 1.0 copy-start.13
  279.8 23.1 %collective-permute-start.27 = (bf16[48,4224]{1,0:T(8,128)(2,1)}, bf16[48,4224]{1,0:T(8,128)(2,1)S(1)}, u32[]{:S(2)}, u32[]{:S(2)}) collective-permute-start(bf16[48,4224]{1,0:T(8,128)(2,1)} %get-tuple-element.116), channel_id=1, source_target_pairs={{0,0},{1,3},{2,2},{3,1},{4,4},{5,7},{6,6},{7,5},{8,8},{9,11},{10,1... | collective-permute-start | bytes 1216520 | tf_op jit(solution)/shard_map/ppermute | solution.py:465
  281.5 21.5 %collective-permute-start.28 = (bf16[48,4224]{1,0:T(8,128)(2,1)}, bf16[48,4224]{1,0:T(8,128)(2,1)S(1)}, u32[]{:S(2)}, u32[]{:S(2)}) collective-permute-start(bf16[48,4224]{1,0:T(8,128)(2,1)} %get-tuple-element.117), channel_id=1, source_target_pairs={{0,4},{1,7},{2,6},{3,5},{4,0},{5,3},{6,2},{7,1},{8,12},{9,15},{10,... | collective-permute-start | bytes 1216520 | tf_op jit(solution)/shard_map/ppermute | solution.py:465
  283.0 20.0 %collective-permute-start.29 = (bf16[48,4224]{1,0:T(8,128)(2,1)}, bf16[48,4224]{1,0:T(8,128)(2,1)S(1)}, u32[]{:S(2)}, u32[]{:S(2)}) collective-permute-start(bf16[48,4224]{1,0:T(8,128)(2,1)} %get-tuple-element.116), channel_id=1, source_target_pairs={{0,1},{1,2},{2,3},{3,0},{4,5},{5,6},{6,7},{7,4},{8,9},{9,10},{10,1... | collective-permute-start | bytes 1216520 | tf_op jit(solution)/shard_map/ppermute | solution.py:465
  284.0 19.1 %collective-permute-start.30 = (bf16[48,4224]{1,0:T(8,128)(2,1)}, bf16[48,4224]{1,0:T(8,128)(2,1)S(1)}, u32[]{:S(2)}, u32[]{:S(2)}) collective-permute-start(bf16[48,4224]{1,0:T(8,128)(2,1)} %get-tuple-element.117), channel_id=1, source_target_pairs={{0,5},{1,6},{2,7},{3,4},{4,1},{5,2},{6,3},{7,0},{8,13},{9,14},{10,... | collective-permute-start | bytes 1216520 | tf_op jit(solution)/shard_map/ppermute | solution.py:465
  303.0 0.8 copy-start.18
  303.0 0.9 copy-start.19
  303.0 1.0 copy-start.20
  303.1 1.1 copy-start.21

commit v3 on v2

--- a/solution.py
+++ b/solution.py
@@ -26,7 +26,15 @@
     return lax.dot_general(a, b, (((0,), (0,)), ((), ())), preferred_element_type=jnp.float32)
 
 
-def pack_kernel(e_ref, x_ref, across_ref, down_ref, rows_in, grads_in, scale_ref, *refs):
+def as_column(row):
+    count = row.shape[1]
+    diagonal = lax.broadcasted_iota(jnp.int32, (count, count), 0) == lax.broadcasted_iota(
+        jnp.int32, (count, count), 1
+    )
+    return jnp.sum(jnp.where(diagonal, row, 0), axis=1, keepdims=True)
+
+
+def pack_kernel(e_ref, x_ref, route_ref, scale_ref, rows_in, grads_in, *refs):
     slot_out, out_refs = refs[0], refs[1:5]
     rows_ref, grads_ref, sems = refs[5:]
     width = rows_ref.shape[1]
@@ -38,34 +46,40 @@
         copy.start()
     count = rows_ref.shape[0]
     size = out_refs[0].shape[0]
-    route = across_ref[...]
+    route = route_ref[...]
     earlier = lax.broadcasted_iota(jnp.int32, (count, count), 0) < lax.broadcasted_iota(
         jnp.int32, (count, count), 1
     )
-    same = (down_ref[...] == route) & earlier
+    same = (as_column(route) == route) & earlier
     rank = jnp.sum(same.astype(jnp.int32), axis=0, keepdims=True)
     other = lax.bitwise_xor(route, e_ref[0])
     slot = (lax.bitwise_xor(other & 1, x_ref[0]) * 2 + (other >> 1)) * size + rank
     slot_out[...] = slot
+    scale = scale_ref[...].astype(jnp.float32)
+    placings = []
+    for group, out_ref in enumerate(out_refs):
+        at = lax.broadcasted_iota(jnp.int32, (size, count), 0) + group * size
+        placing = (at == slot).astype(jnp.float32)
+        placings.append(placing.astype(jnp.bfloat16))
+        placed = jnp.sum(placing * scale, axis=1, keepdims=True)
+        out_ref[:, 2 * width :] = jnp.broadcast_to(placed, (size, LANES)).astype(jnp.bfloat16)
     for copy in copies:
         copy.wait()
-    for group, out_ref in enumerate(out_refs):
-        at = lax.broadcasted_iota(jnp.int32, (size, count), 0) + group * size
-        placing = (at == slot).astype(jnp.float32).astype(jnp.bfloat16)
-        for start, ref in ((0, rows_ref), (width, grads_ref), (2 * width, scale_ref)):
-            out_ref[:, start : start + ref.shape[1]] = jnp.dot(
+    for placing, out_ref in zip(placings, out_refs, strict=True):
+        for start, ref in ((0, rows_ref), (width, grads_ref)):
+            out_ref[:, start : start + width] = jnp.dot(
                 placing, ref[...], preferred_element_type=jnp.float32
             ).astype(jnp.bfloat16)
 
 
-def pack(e, x, routing, rows, grads, scale, size):
+def pack(e, x, route, scale, rows, grads, size):
     count, width = rows.shape
     scalar = pl.BlockSpec(memory_space=pltpu.SMEM)
     inside = pl.BlockSpec(memory_space=pltpu.VMEM)
     anywhere = pl.BlockSpec(memory_space=pl.ANY)
     return pl.pallas_call(
         pack_kernel,
-        in_specs=[scalar, scalar, inside, inside, anywhere, anywhere, inside],
+        in_specs=[scalar, scalar, inside, inside, anywhere, anywhere],
         out_specs=[inside] * 5,
         out_shape=[jax.ShapeDtypeStruct((1, count), jnp.int32)]
         + [jax.ShapeDtypeStruct((size, 2 * width + LANES), jnp.bfloat16)] * 4,
@@ -76,7 +90,7 @@
         ],
         compiler_params=pltpu.CompilerParams(vmem_limit_bytes=VMEM),
         cost_estimate=SMALL,
-    )(e, x, routing.reshape(1, count), routing, rows, grads, scale)
+    )(e, x, route, scale, rows, grads)
 
 
 def nothing_kernel(*refs):
@@ -222,14 +236,10 @@
     weight_copy(0, 2).start()
     for k in range(3):
         weight_copy(1, k).start()
-    total_ref[...] = jnp.zeros_like(total_ref)
     scale_sum_ref[...] = jnp.zeros_like(scale_sum_ref)
     for copy in row_copies + grad_copies:
         copy.wait()
-    scale = scale_ref[:, 0:1].astype(jnp.float32)
-    scaled_ref[...] = (scale * grads_ref[...].astype(jnp.float32)).astype(jnp.bfloat16)
     scaled_copy = pltpu.make_async_copy(scaled_ref, scaled_out, scaled_sem)
-    scaled_copy.start()
 
     def products(i):
         held = held_ref.at[lax.rem(i, slots)]
@@ -278,7 +288,12 @@
                 weight_copy(i + 2, k).start()
 
     arrive(0)
-    activate(0, *products(0))
+    first_products = products(0)
+    total_ref[...] = jnp.zeros_like(total_ref)
+    scale = scale_ref[:, 0:1].astype(jnp.float32)
+    scaled_ref[...] = (scale * grads_ref[...].astype(jnp.float32)).astype(jnp.bfloat16)
+    activate(0, *first_products)
+    scaled_copy.start()
     for k in range(3):
         act_copy(0, k).start()
 
@@ -409,7 +424,7 @@
 def unpack_kernel(slot_ref, *refs):
     grads_ref, scale_ref = refs[-2:]
     width = grads_ref.shape[1]
-    slot = slot_ref[...]
+    slot = as_column(slot_ref[...])
     total = jnp.zeros((slot.shape[0], width + LANES), jnp.float32)
     for group, ref in enumerate(refs[:-2]):
         size = ref.shape[0]
@@ -422,7 +437,7 @@
 
 
 def unpack(order, slot, groups, width):
-    rows = slot.shape[0]
+    rows = slot.shape[1]
     inside = pl.BlockSpec(memory_space=pltpu.VMEM)
     return order.call(
         unpack_kernel,
@@ -445,14 +460,13 @@
     w_gate, w_up, w_down = gate_weight[0], up_weight[0], down_weight[0]
     lane = ((z * 2 + x) * 2).astype(jnp.int32).reshape(1)
 
-    scale_lanes = jnp.broadcast_to(gate_scale[:, None], (local_rows, LANES))
     slot, *groups = pack(
         e.astype(jnp.int32).reshape(1),
         x.astype(jnp.int32).reshape(1),
-        routing,
+        routing.reshape(1, local_rows),
+        gate_scale.reshape(1, local_rows),
         token_rows,
         row_grads,
-        scale_lanes,
         size,
     )
 
@@ -542,7 +556,7 @@
     near_back = [over_expert(near_own, 0), over_expert(near_own, 0, 1)]
     (grad_down,) = grads_of(scaled, "hidden")
     input_grads, scale_grads = unpack(
-        order, slot.reshape(-1, 1), [near_back[0], far_back[0], near_back[1], far_back[1]], width
+        order, slot, [near_back[0], far_back[0], near_back[1], far_back[1]], width
     )
     return (input_grads, scale_grads[0], grad_gate[None], grad_up[None], grad_down[None])
 

time: 309 us -> 307 us (level)
  starting transfers between devices: 49.9 us -> 57 us
  waiting for transfers between devices: 49.3 us -> 43 us
    ppermute x14, waiting for transfers between devices: 44.4 us -> 22.6 us  [along(): return lax.ppermute(a, 'dp', pairs)]
    ppermute x8, waiting for transfers between devices: 0.08 us -> 17.2 us  [over_expert(): return lax.ppermute(a, ('expert', 'etensor'), pairs)]
    ppermute x9, starting transfers between devices: 18.6 us -> 25.9 us  [across(): return lax.ppermute(a, 'etensor', ((0, 1), (1, 0)))]
    unnamed x57 -> x54, local copies, waits for them, and re-layouts: 12.3 us -> 11.7 us
  transfers between devices with their start and end apart: 31 -> 31, of which waited for: 7 -> 6; matrix products, arithmetic and copies ran while one was open for 0% -> 0% of each run, Pallas kernels for 58% -> 58%
where the time goes in v3:
time: 307 us
  Pallas kernels  193 us (63%)
  starting transfers between devices  57 us (19%)
  waiting for transfers between devices  43 us (14%)
  local copies, waits for them, and re-layouts  12.3 us (4%)
    pallas_call x17, Pallas kernels, call(): pl.pallas_call(body, in_specs=[*in_specs, anywhere], out_specs=[*out_spec...  189 us
    ppermute x9, starting transfers between devices, across(): return lax.ppermute(a, 'etensor', ((0, 1), (1, 0)))  25.9 us
    ppermute x14, waiting for transfers between devices, along(): return lax.ppermute(a, 'dp', pairs)  22.6 us
    ppermute x14, starting transfers between devices, along(): return lax.ppermute(a, 'dp', pairs)  20.1 us
    ppermute x8, waiting for transfers between devices, over_expert(): return lax.ppermute(a, ('expert', 'etensor'), pairs)  17.2 us
    unnamed x54, local copies, waits for them, and re-layouts  11.7 us
    ppermute x8, starting transfers between devices, over_expert(): return lax.ppermute(a, ('expert', 'etensor'), pairs)  11 us
  transfers between devices with their start and end apart: 31, of which 6 were waited for; matrix products, arithmetic and copies ran while one was open for 0% of the time, Pallas kernels for 58%

profile of v3, /device:TPU:0, one launch (start us, length us, event | category | flops | bytes accessed | tf_op | source)
XLA Modules:
  0.0 306.8 jit_solution(2820826103051887136)
XLA Ops:
  0.6 4.5 %shard_map.110 = (s32[1,128]{1,0:T(1,128)}, bf16[48,8320]{1,0:T(8,128)(2,1)}, bf16[48,8320]{1,0:T(8,128)(2,1)}, bf16[48,8320]{1,0:T(8,128)(2,1)}, bf16[48,8320]{1,0:T(8,128)(2,1)}) custom-call(s32[1]{0:T(128)} %bitcast.e_ref, s32[1]{0:T(128)} %bitcast.1.x_ref, s32[1,128]{1,0:T(1,128)} %bitcast.25, bf16[1,128]{1,0:T(2,128)(2,1)} %bitcast.26, ...), custom_call_target="tpu_custom_call" | custom-call | tf_op jit(solution)/shard_map/pallas_call | solution.py:80
  5.1 1.8 collective-permute-start
  6.9 3.0 collective-permute-start.5
  9.9 1.6 collective-permute-start.4
  11.5 1.9 collective-permute-start.1
  13.5 14.3 %collective-permute-done.5.refs_0_.refs_1_.refs_4_ = bf16[48,8320]{1,0:T(8,128)(2,1)S(1)} collective-permute-done((bf16[48,8320]{1,0:T(8,128)(2,1)S(1)}, bf16[48,8320]{1,0:T(8,128)(2,1)S(1)}, u32[]{:S(2)}, u32[]{:S(2)}) %collective-permute-start.5) | collective-permute-done | bytes 798752 | tf_op jit(solution)/shard_map/ppermute | solution.py:482
  27.7 1.6 collective-permute-start.6
  29.3 1.7 collective-permute-start.2
  31.0 1.3 collective-permute-start.9
  32.4 4.4 %collective-permute-start.8 = (bf16[48,8320]{1,0:T(8,128)(2,1)S(1)}, bf16[48,8320]{1,0:T(8,128)(2,1)}, u32[]{:S(2)}, u32[]{:S(2)}) collective-permute-start(bf16[48,8320]{1,0:T(8,128)(2,1)S(1)} %collective-permute-done.5.refs_0_.refs_1_.refs_4_), channel_id=1, source_target_pairs={{0,1},{1,0},{2,3},{3,2},{4,5},{5,4},{6,7},{7,6},{8,9},{9,8},{10,11... | collective-permute-start | bytes 2396168 | tf_op jit(solution)/shard_map/ppermute | solution.py:485
  36.8 1.3 collective-permute-start.7
  38.1 12.2 %collective-permute-done.2.refs_3_.refs_2_ = bf16[48,8320]{1,0:T(8,128)(2,1)S(1)} collective-permute-done((bf16[48,8320]{1,0:T(8,128)(2,1)}, bf16[48,8320]{1,0:T(8,128)(2,1)S(1)}, u32[]{:S(2)}, u32[]{:S(2)}) %collective-permute-start.2) | collective-permute-done | bytes 798752 | tf_op jit(solution)/shard_map/ppermute | solution.py:479
  50.2 0.6 broadcast_in_dim.12.refs_4_
  50.9 0.3 copy-done
  51.2 3.2 %collective-permute-done.9.refs_2_ = bf16[48,8320]{1,0:T(8,128)(2,1)} collective-permute-done((bf16[48,8320]{1,0:T(8,128)(2,1)}, bf16[48,8320]{1,0:T(8,128)(2,1)}, u32[]{:S(2)}, u32[]{:S(2)}) %collective-permute-start.9) | collective-permute-done | bytes 798752 | tf_op jit(solution)/shard_map/ppermute | solution.py:482
  54.3 2.3 shard_map.112
  56.7 3.0 collective-permute-start.10
  59.6 5.0 %collective-permute-done.3.refs_5_.refs_4_.refs_3_ = bf16[48,8320]{1,0:T(8,128)(2,1)S(1)} collective-permute-done((bf16[48,8320]{1,0:T(8,128)(2,1)}, bf16[48,8320]{1,0:T(8,128)(2,1)S(1)}, u32[]{:S(2)}, u32[]{:S(2)}) %collective-permute-start.3) | collective-permute-done | bytes 798752 | tf_op jit(solution)/shard_map/ppermute | solution.py:479
  64.6 5.1 %collective-permute-done.7.refs_2_ = bf16[48,8320]{1,0:T(8,128)(2,1)} collective-permute-done((bf16[48,8320]{1,0:T(8,128)(2,1)}, bf16[48,8320]{1,0:T(8,128)(2,1)}, u32[]{:S(2)}, u32[]{:S(2)}) %collective-permute-start.7) | collective-permute-done | bytes 798752 | tf_op jit(solution)/shard_map/ppermute | solution.py:482
  69.7 2.8 shard_map.113
  72.5 2.6 collective-permute-start.12
  75.1 5.5 %collective-permute-start.11 = (bf16[48,8320]{1,0:T(8,128)(2,1)}, bf16[48,8320]{1,0:T(8,128)(2,1)S(1)}, u32[]{:S(2)}, u32[]{:S(2)}) collective-permute-start(bf16[48,8320]{1,0:T(8,128)(2,1)} %get-tuple-element.78.refs_5_.refs_8_), channel_id=1, source_target_pairs={{0,1},{1,0},{2,3},{3,2},{4,5},{5,4},{6,7},{7,6},{8,9},{9,8},{10,11... | collective-permute-start | bytes 2396168 | tf_op jit(solution)/shard_map/ppermute | solution.py:485
  80.6 28.8 %shard_map.114 = (bf16[192,1792]{1,0:T(8,128)(2,1)}, bf16[192,1792]{1,0:T(8,128)(2,1)}, bf16[192,1792]{1,0:T(8,128)(2,1)}, bf16[192,4096]{1,0:T(8,128)(2,1)}, bf...) custom-call(s32[1]{0:T(128)} %bitcast.4.refs_0_, ...), custom_call_target="tpu_custom_call", output_to_operand_aliasing={{7}: (8, {})} | custom-call | tf_op jit(solution)/shard_map/pallas_call | solution.py:113
  109.5 0.8 copy-done.4
  110.6 0.3 copy-done.17
  110.9 3.2 %shard_map.115 = (bf16[48,8320]{1,0:T(8,128)(2,1)}, bf16[48,8320]{1,0:T(8,128)(2,1)}, bf16[48,8320]{1,0:T(8,128)(2,1)}, f32[8,128]{1,0:T(8,128)}) custom-call(s32[1]{0:T(128)} %bitcast.8.refs_0_, bf16[48,8320]{1,0:T(8,128)(2,1)} %copy-done.17, bf16[48,8320]{1,0:T(8,128)(2,1)} %copy-done.15, ...), custom_call_target="tpu_custom_call", output_to_operand_aliasing={{3}: (5, {})} | custom-call | tf_op jit(solution)/shard_map/pallas_call | solution.py:113
  114.0 0.8 collective-permute-start.17
  114.8 7.3 %collective-permute-start.18 = (bf16[48,8320]{1,0:T(8,128)(2,1)}, bf16[48,8320]{1,0:T(8,128)(2,1)S(1)}, u32[]{:S(2)}, u32[]{:S(2)}) collective-permute-start(bf16[48,8320]{1,0:T(8,128)(2,1)} %get-tuple-element.87.refs_1_.refs_10_), channel_id=1, source_target_pairs={{0,1},{1,0},{2,3},{3,2},{4,5},{5,4},{6,7},{7,6},{8,9},{9,8},{10,11... | collective-permute-start | bytes 2396168 | tf_op jit(solution)/shard_map/ppermute | solution.py:485
  122.2 0.9 copy-done.10
  123.1 33.1 %shard_map.116 = (bf16[288,1792]{1,0:T(8,128)(2,1)}, bf16[288,1792]{1,0:T(8,128)(2,1)}, bf16[288,1792]{1,0:T(8,128)(2,1)}, bf16[288,4096]{1,0:T(8,128)(2,1)}, bf...) custom-call(s32[1]{0:T(128)} %bitcast.4.refs_0_, ...), custom_call_target="tpu_custom_call", output_to_operand_aliasing={{7}: (10, {})} | custom-call | tf_op jit(solution)/shard_map/pallas_call | solution.py:113
  156.1 0.6 collective-permute-start.14
  156.7 1.9 collective-permute-start.16
  158.7 0.9 copy-done.16
  159.8 2.1 shard_map.117
  161.9 2.0 collective-permute-start.19
  163.9 0.9 copy-done.11
  164.9 28.6 %shard_map.118 = (bf16[192,1792]{1,0:T(8,128)(2,1)}, bf16[192,1792]{1,0:T(8,128)(2,1)}, bf16[192,1792]{1,0:T(8,128)(2,1)}, bf16[192,4096]{1,0:T(8,128)(2,1)}, bf...) custom-call(s32[1]{0:T(128)} %bitcast.4.refs_0_, ...), custom_call_target="tpu_custom_call", output_to_operand_aliasing={{6}: (8, {})} | custom-call | tf_op jit(solution)/shard_map/pallas_call | solution.py:113
  193.5 1.1 collective-permute-start.15
  194.6 0.9 copy-done.6
  195.5 0.3 copy-done.7
  195.9 0.9 copy-done.8
  196.7 25.5 %shard_map.120 = (bf16[96,1792]{1,0:T(8,128)(2,1)}, bf16[96,1792]{1,0:T(8,128)(2,1)}, bf16[96,1792]{1,0:T(8,128)(2,1)}, bf16[96,4096]{1,0:T(8,128)(2,1)}, bf16[4...) custom-call(s32[1]{0:T(128)} %bitcast.4.refs_0_, ...), custom_call_target="tpu_custom_call", output_to_operand_aliasing={{6}: (6, {})} | custom-call | tf_op jit(solution)/shard_map/pallas_call | solution.py:113
  222.3 2.0 collective-permute-start.21
  224.3 0.9 copy-done.14
  225.2 2.4 shard_map.121
  227.6 3.3 %collective-permute-done.21.refs_1_ = bf16[48,4224]{1,0:T(8,128)(2,1)S(1)} collective-permute-done((bf16[48,4224]{1,0:T(8,128)(2,1)}, bf16[48,4224]{1,0:T(8,128)(2,1)S(1)}, u32[]{:S(2)}, u32[]{:S(2)}) %collective-permute-start.21) | collective-permute-done | bytes 405536 | tf_op jit(solution)/shard_map/ppermute | solution.py:485
  230.8 0.7 copy-done.22
  231.6 2.0 shard_map.122
  233.6 0.9 copy-done.12
  234.5 3.3 %shard_map.123 = (bf16[48,4224]{1,0:T(8,128)(2,1)}, bf16[96,4224]{1,0:T(8,128)(2,1)}, f32[8,128]{1,0:T(8,128)}) custom-call(bf16[96,4224]{1,0:T(8,128)(2,1)} %get-tuple-element.76.refs_0_, bf16[96,4224]{1,0:T(8,128)(2,1)} %copy-done.6, bf16[96,4224]{1,0:T(8,128)(2,1)} %copy-done.12, bf16[96,4224]{1,0:T(8,128)(2,1)} %copy-done.7, ...), custom_call_target="tpu_custom_call", output_to_operand_aliasing={{2}: (5, {})} | custom-call | tf_op jit(solution)/shard_map/pallas_call | solution.py:113
  237.8 1.7 collective-permute-start.23
  239.5 1.4 collective-permute-start.24
  240.9 1.7 collective-permute-start.25
  242.5 1.3 collective-permute-start.26
  243.9 30.2 %shard_map.124 = (bf16[1792,4096]{1,0:T(8,128)(2,1)}, bf16[1792,4096]{1,0:T(8,128)(2,1)}, f32[8,128]{1,0:T(8,128)}) custom-call(bf16[48,8320]{1,0:T(8,128)(2,1)} %copy-done.9, bf16[48,8320]{1,0:T(8,128)(2,1)} %copy-done.2, bf16[48,8320]{1,0:T(8,128)(2,1)} %copy-done, bf16[48,8320]{1,0:T(8,128)(2,1)} %copy-done.3, ...), custom_call_target="tpu_custom_call", output_to_operand_aliasing={{2}: (24, {})} | custom-call | tf_op jit(solution)/shard_map/pallas_call | solution.py:113
  274.1 0.7 copy-done.23
  275.3 2.8 shard_map.125
  278.2 0.4 collective-permute-start.29
  278.5 1.6 collective-permute-start.27
  280.2 1.6 collective-permute-start.30
  281.8 2.0 collective-permute-start.28
  283.7 18.2 %shard_map.126 = (bf16[1792,4096]{1,0:T(8,128)(2,1)}, f32[8,128]{1,0:T(8,128)}) custom-call(bf16[192,4096]{1,0:T(8,128)(2,1)} %get-tuple-element.118.refs_0_, bf16[288,4096]{1,0:T(8,128)(2,1)} %get-tuple-element.119.refs_1_, bf16[192,4096]{1,0:T(8,128)(2,1)} %get-tuple-element.120.refs_2_, ...), custom_call_target="tpu_custom_call", output_to_operand_aliasing={{1}: (8, {})} | custom-call | tf_op jit(solution)/shard_map/pallas_call | solution.py:113
  302.0 0.7 copy-done.18
  303.1 3.7 %shard_map.127 = (bf16[128,4096]{1,0:T(8,128)(2,1)}, f32[1,128]{1,0:T(1,128)}, f32[8,128]{1,0:T(8,128)}) custom-call(s32[1,128]{1,0:T(1,128)} %get-tuple-element.69.refs_0_, bf16[48,4224]{1,0:T(8,128)(2,1)} %copy-done.19, bf16[48,4224]{1,0:T(8,128)(2,1)} %copy-done.21, bf16[48,4224]{1,0:T(8,128)(2,1)} %copy-done.18, ...), custom_call_target="tpu_custom_call", output_to_operand_aliasing={{2}: (5, {})} | custom-call | tf_op jit(solution)/shard_map/pallas_call | solution.py:113
  (71 shorter events, 1.8 us)
Async XLA Ops:
  5.1 1.8 collective-permute-start
  6.9 29.8 %copy-start.9 = (bf16[48,8320]{1,0:T(8,128)(2,1)}, bf16[48,8320]{1,0:T(8,128)(2,1)S(1)}, u32[]{:S(2)}) copy-start(bf16[48,8320]{1,0:T(8,128)(2,1)S(1)} %collective-permute-done.refs_1_.refs_0_) | copy-start | bytes 2396164
  6.9 20.8 %collective-permute-start.5 = (bf16[48,8320]{1,0:T(8,128)(2,1)S(1)}, bf16[48,8320]{1,0:T(8,128)(2,1)S(1)}, u32[]{:S(2)}, u32[]{:S(2)}) collective-permute-start(bf16[48,8320]{1,0:T(8,128)(2,1)S(1)} %collective-permute-done.refs_1_.refs_0_), channel_id=1, source_target_pairs={{0,8},{8,0},{16,24},{24,16},{1,9},{9,1},{17,25},{25,17},{2,10},{10... | collective-permute-start | bytes 2396168 | tf_op jit(solution)/shard_map/ppermute | solution.py:482
  9.9 21.1 %collective-permute-start.4 = (bf16[48,8320]{1,0:T(8,128)(2,1)S(1)}, bf16[48,8320]{1,0:T(8,128)(2,1)}, u32[]{:S(2)}, u32[]{:S(2)}) collective-permute-start(bf16[48,8320]{1,0:T(8,128)(2,1)S(1)} %collective-permute-done.refs_1_.refs_0_), channel_id=1, source_target_pairs={{8,16},{16,8},{9,17},{17,9},{10,18},{18,10},{11,19},{19,11},{12,20... | collective-permute-start | bytes 2396168 | tf_op jit(solution)/shard_map/ppermute | solution.py:482
  11.5 20.8 %collective-permute-start.1 = (bf16[48,8320]{1,0:T(8,128)(2,1)}, bf16[48,8320]{1,0:T(8,128)(2,1)S(1)}, u32[]{:S(2)}, u32[]{:S(2)}) collective-permute-start(bf16[48,8320]{1,0:T(8,128)(2,1)} %get-tuple-element.71), channel_id=1, source_target_pairs={{0,2},{1,1},{2,0},{3,3},{4,6},{5,5},{6,4},{7,7},{8,10},{9,9},{10,8... | collective-permute-start | bytes 2396168 | tf_op jit(solution)/shard_map/ppermute | solution.py:479
  27.7 23.1 %copy-start.1 = (bf16[48,8320]{1,0:T(8,128)(2,1)}, bf16[48,8320]{1,0:T(8,128)(2,1)S(1)}, u32[]{:S(2)}) copy-start(bf16[48,8320]{1,0:T(8,128)(2,1)S(1)} %collective-permute-done.5.refs_0_.refs_1_.refs_4_) | copy-start | bytes 2396164
  27.7 9.0 %collective-permute-start.6 = (bf16[48,8320]{1,0:T(8,128)(2,1)S(1)}, bf16[48,8320]{1,0:T(8,128)(2,1)}, u32[]{:S(2)}, u32[]{:S(2)}) collective-permute-start(bf16[48,8320]{1,0:T(8,128)(2,1)S(1)} %collective-permute-done.5.refs_0_.refs_1_.refs_4_), channel_id=1, source_target_pairs={{8,16},{16,8},{9,17},{17,9},{10,18},{18,10},{11,19},{19,11},{12,20... | collective-permute-start | bytes 2396168 | tf_op jit(solution)/shard_map/ppermute | solution.py:482
  29.3 21.0 %collective-permute-start.2 = (bf16[48,8320]{1,0:T(8,128)(2,1)}, bf16[48,8320]{1,0:T(8,128)(2,1)S(1)}, u32[]{:S(2)}, u32[]{:S(2)}) collective-permute-start(bf16[48,8320]{1,0:T(8,128)(2,1)} %get-tuple-element.72), channel_id=1, source_target_pairs={{0,4},{1,7},{2,6},{3,5},{4,0},{5,3},{6,2},{7,1},{8,12},{9,15},{10,... | collective-permute-start | bytes 2396168 | tf_op jit(solution)/shard_map/ppermute | solution.py:479
  31.0 23.3 %collective-permute-start.9 = (bf16[48,8320]{1,0:T(8,128)(2,1)}, bf16[48,8320]{1,0:T(8,128)(2,1)}, u32[]{:S(2)}, u32[]{:S(2)}) collective-permute-start(bf16[48,8320]{1,0:T(8,128)(2,1)} %collective-permute-done.4.refs_1_), channel_id=1, source_target_pairs={{8,0},{16,24},{9,1},{17,25},{10,2},{18,26},{11,3},{19,27},{12,4},{... | collective-permute-start | bytes 2396168 | tf_op jit(solution)/shard_map/ppermute | solution.py:482
  32.3 32.3 %collective-permute-start.3 = (bf16[48,8320]{1,0:T(8,128)(2,1)}, bf16[48,8320]{1,0:T(8,128)(2,1)S(1)}, u32[]{:S(2)}, u32[]{:S(2)}) collective-permute-start(bf16[48,8320]{1,0:T(8,128)(2,1)} %get-tuple-element.73), channel_id=1, source_target_pairs={{0,6},{1,5},{2,4},{3,7},{4,2},{5,1},{6,0},{7,3},{8,14},{9,13},{10,... | collective-permute-start | bytes 2396168 | tf_op jit(solution)/shard_map/ppermute | solution.py:479
  32.4 18.5 %copy-start.2 = (bf16[48,8320]{1,0:T(8,128)(2,1)}, bf16[48,8320]{1,0:T(8,128)(2,1)S(1)}, u32[]{:S(2)}) copy-start(bf16[48,8320]{1,0:T(8,128)(2,1)S(1)} %collective-permute-done.1.refs_2_.refs_1_) | copy-start | bytes 2396164
  32.4 32.2 %collective-permute-start.8 = (bf16[48,8320]{1,0:T(8,128)(2,1)S(1)}, bf16[48,8320]{1,0:T(8,128)(2,1)}, u32[]{:S(2)}, u32[]{:S(2)}) collective-permute-start(bf16[48,8320]{1,0:T(8,128)(2,1)S(1)} %collective-permute-done.5.refs_0_.refs_1_.refs_4_), channel_id=1, source_target_pairs={{0,1},{1,0},{2,3},{3,2},{4,5},{5,4},{6,7},{7,6},{8,9},{9,8},{10,11... | collective-permute-start | bytes 2396168 | tf_op jit(solution)/shard_map/ppermute | solution.py:485
  36.8 33.0 %collective-permute-start.7 = (bf16[48,8320]{1,0:T(8,128)(2,1)}, bf16[48,8320]{1,0:T(8,128)(2,1)}, u32[]{:S(2)}, u32[]{:S(2)}) collective-permute-start(bf16[48,8320]{1,0:T(8,128)(2,1)} %collective-permute-done.6.refs_1_), channel_id=1, source_target_pairs={{8,0},{16,24},{9,1},{17,25},{10,2},{18,26},{11,3},{19,27},{12,4},{... | collective-permute-start | bytes 2396168 | tf_op jit(solution)/shard_map/ppermute | solution.py:482
  50.2 0.9 copy-start
  56.7 52.8 %collective-permute-start.10 = (bf16[48,8320]{1,0:T(8,128)(2,1)}, bf16[48,8320]{1,0:T(8,128)(2,1)S(1)}, u32[]{:S(2)}, u32[]{:S(2)}) collective-permute-start(bf16[48,8320]{1,0:T(8,128)(2,1)} %get-tuple-element.77.refs_3_.refs_6_), channel_id=1, source_target_pairs={{0,1},{1,0},{2,3},{3,2},{4,5},{5,4},{6,7},{7,6},{8,9},{9,8},{10,11... | collective-permute-start | bytes 2396168 | tf_op jit(solution)/shard_map/ppermute | solution.py:485
  64.6 5.1 %copy-start.3 = (bf16[48,8320]{1,0:T(8,128)(2,1)}, bf16[48,8320]{1,0:T(8,128)(2,1)S(1)}, u32[]{:S(2)}) copy-start(bf16[48,8320]{1,0:T(8,128)(2,1)S(1)} %collective-permute-done.3.refs_5_.refs_4_.refs_3_) | copy-start | bytes 2396164
  72.5 36.9 %collective-permute-start.13 = (bf16[48,8320]{1,0:T(8,128)(2,1)}, bf16[48,8320]{1,0:T(8,128)(2,1)S(1)}, u32[]{:S(2)}, u32[]{:S(2)}) collective-permute-start(bf16[48,8320]{1,0:T(8,128)(2,1)} %get-tuple-element.79), channel_id=1, source_target_pairs={{0,8},{8,0},{16,24},{24,16},{1,9},{9,1},{17,25},{25,17},{2,10},{10... | collective-permute-start | bytes 2396168 | tf_op jit(solution)/shard_map/ppermute | solution.py:482
  72.5 36.9 %collective-permute-start.12 = (bf16[48,8320]{1,0:T(8,128)(2,1)}, bf16[48,8320]{1,0:T(8,128)(2,1)S(1)}, u32[]{:S(2)}, u32[]{:S(2)}) collective-permute-start(bf16[48,8320]{1,0:T(8,128)(2,1)} %get-tuple-element.79), channel_id=1, source_target_pairs={{0,24},{8,16},{16,8},{24,0},{1,25},{9,17},{17,9},{25,1},{2,26},{10... | collective-permute-start | bytes 2396168 | tf_op jit(solution)/shard_map/ppermute | solution.py:482
  75.1 47.0 %collective-permute-start.11 = (bf16[48,8320]{1,0:T(8,128)(2,1)}, bf16[48,8320]{1,0:T(8,128)(2,1)S(1)}, u32[]{:S(2)}, u32[]{:S(2)}) collective-permute-start(bf16[48,8320]{1,0:T(8,128)(2,1)} %get-tuple-element.78.refs_5_.refs_8_), channel_id=1, source_target_pairs={{0,1},{1,0},{2,3},{3,2},{4,5},{5,4},{6,7},{7,6},{8,9},{9,8},{10,11... | collective-permute-start | bytes 2396168 | tf_op jit(solution)/shard_map/ppermute | solution.py:485
  109.4 0.9 copy-start.4
  109.5 1.1 copy-start.15
  109.5 1.4 copy-start.17
  114.0 44.6 %collective-permute-start.17 = (bf16[48,8320]{1,0:T(8,128)(2,1)}, bf16[48,8320]{1,0:T(8,128)(2,1)S(1)}, u32[]{:S(2)}, u32[]{:S(2)}) collective-permute-start(bf16[48,8320]{1,0:T(8,128)(2,1)} %get-tuple-element.86), channel_id=1, source_target_pairs={{0,16},{8,24},{16,0},{24,8},{1,17},{9,25},{17,1},{25,9},{2,18},{10... | collective-permute-start | bytes 2396168 | tf_op jit(solution)/shard_map/ppermute | solution.py:482
  114.8 43.9 %collective-permute-start.18 = (bf16[48,8320]{1,0:T(8,128)(2,1)}, bf16[48,8320]{1,0:T(8,128)(2,1)S(1)}, u32[]{:S(2)}, u32[]{:S(2)}) collective-permute-start(bf16[48,8320]{1,0:T(8,128)(2,1)} %get-tuple-element.87.refs_1_.refs_10_), channel_id=1, source_target_pairs={{0,1},{1,0},{2,3},{3,2},{4,5},{5,4},{6,7},{7,6},{8,9},{9,8},{10,11... | collective-permute-start | bytes 2396168 | tf_op jit(solution)/shard_map/ppermute | solution.py:485
  122.1 41.8 %collective-permute-start.20 = (bf16[48,8320]{1,0:T(8,128)(2,1)}, bf16[48,8320]{1,0:T(8,128)(2,1)S(1)}, u32[]{:S(2)}, u32[]{:S(2)}) collective-permute-start(bf16[48,8320]{1,0:T(8,128)(2,1)} %get-tuple-element.90.refs_2_.refs_11_), channel_id=1, source_target_pairs={{0,1},{1,0},{2,3},{3,2},{4,5},{5,4},{6,7},{7,6},{8,9},{9,8},{10,11... | collective-permute-start | bytes 2396168 | tf_op jit(solution)/shard_map/ppermute | solution.py:485
  122.2 0.9 copy-start.10
  156.1 38.5 %collective-permute-start.14 = (bf16[96,4224]{1,0:T(8,128)(2,1)}, bf16[96,4224]{1,0:T(8,128)(2,1)S(1)}, u32[]{:S(2)}, u32[]{:S(2)}) collective-permute-start(bf16[96,4224]{1,0:T(8,128)(2,1)} %get-tuple-element.82), channel_id=1, source_target_pairs={{0,8},{8,0},{16,24},{24,16},{1,9},{9,1},{17,25},{25,17},{2,10},{10... | collective-permute-start | bytes 2433032 | tf_op jit(solution)/shard_map/ppermute | solution.py:482
  156.7 37.9 %collective-permute-start.16 = (bf16[96,4224]{1,0:T(8,128)(2,1)}, bf16[96,4224]{1,0:T(8,128)(2,1)S(1)}, u32[]{:S(2)}, u32[]{:S(2)}) collective-permute-start(bf16[96,4224]{1,0:T(8,128)(2,1)} %get-tuple-element.84), channel_id=1, source_target_pairs={{0,24},{8,16},{16,8},{24,0},{1,25},{9,17},{17,9},{25,1},{2,26},{10... | collective-permute-start | bytes 2433032 | tf_op jit(solution)/shard_map/ppermute | solution.py:482
  158.7 0.9 copy-start.16
  158.7 1.1 copy-start.5
  161.9 33.9 %collective-permute-start.19 = (bf16[48,8320]{1,0:T(8,128)(2,1)}, bf16[48,8320]{1,0:T(8,128)(2,1)S(1)}, u32[]{:S(2)}, u32[]{:S(2)}) collective-permute-start(bf16[48,8320]{1,0:T(8,128)(2,1)} %get-tuple-element.89.refs_1_.refs_14_), channel_id=1, source_target_pairs={{0,1},{1,0},{2,3},{3,2},{4,5},{5,4},{6,7},{7,6},{8,9},{9,8},{10,11... | collective-permute-start | bytes 2396168 | tf_op jit(solution)/shard_map/ppermute | solution.py:485
  163.9 0.9 copy-start.11
  164.9 28.7 %copy-start.26 = (bf16[96,4224]{1,0:T(8,128)(2,1)S(1)}, bf16[96,4224]{1,0:T(8,128)(2,1)}, u32[]{:S(2)}) copy-start(bf16[96,4224]{1,0:T(8,128)(2,1)} %get-tuple-element.83) | copy-start | bytes 2433028
  193.4 30.8 %collective-permute-start.22 = (bf16[96,4224]{1,0:T(8,128)(2,1)}, bf16[96,4224]{1,0:T(8,128)(2,1)S(1)}, u32[]{:S(2)}, u32[]{:S(2)}) collective-permute-start(bf16[96,4224]{1,0:T(8,128)(2,1)} %get-tuple-element.96), channel_id=1, source_target_pairs={{0,1},{1,0},{2,3},{3,2},{4,5},{5,4},{6,7},{7,6},{8,9},{9,8},{10,11... | collective-permute-start | bytes 2433032 | tf_op jit(solution)/shard_map/ppermute | solution.py:485
  193.5 40.0 %collective-permute-start.15 = (bf16[96,4224]{1,0:T(8,128)(2,1)S(1)}, bf16[96,4224]{1,0:T(8,128)(2,1)S(1)}, u32[]{:S(2)}, u32[]{:S(2)}) collective-permute-start(bf16[96,4224]{1,0:T(8,128)(2,1)S(1)} %copy-done.26), channel_id=1, source_target_pairs={{0,16},{8,24},{16,0},{24,8},{1,17},{9,25},{17,1},{25,9},{2,18},{10... | collective-permute-start | bytes 2433032 | tf_op jit(solution)/shard_map/ppermute | solution.py:482
  194.6 0.9 copy-start.6
  194.6 1.2 copy-start.7
  195.8 0.9 copy-start.8
  222.3 8.6 %collective-permute-start.21 = (bf16[48,4224]{1,0:T(8,128)(2,1)}, bf16[48,4224]{1,0:T(8,128)(2,1)S(1)}, u32[]{:S(2)}, u32[]{:S(2)}) collective-permute-start(bf16[48,4224]{1,0:T(8,128)(2,1)} %get-tuple-element.94), channel_id=1, source_target_pairs={{0,1},{1,0},{2,3},{3,2},{4,5},{5,4},{6,7},{7,6},{8,9},{9,8},{10,11... | collective-permute-start | bytes 1216520 | tf_op jit(solution)/shard_map/ppermute | solution.py:485
  224.3 0.9 copy-start.14
  230.8 0.7 copy-start.22
  233.6 0.9 copy-start.12
  237.8 36.3 %collective-permute-start.23 = (bf16[96,4224]{1,0:T(8,128)(2,1)}, bf16[96,4224]{1,0:T(8,128)(2,1)S(1)}, u32[]{:S(2)}, u32[]{:S(2)}) collective-permute-start(bf16[96,4224]{1,0:T(8,128)(2,1)} %get-tuple-element.101), channel_id=1, source_target_pairs={{0,1},{1,0},{2,3},{3,2},{4,5},{5,4},{6,7},{7,6},{8,9},{9,8},{10,11... | collective-permute-start | bytes 2433032 | tf_op jit(solution)/shard_map/ppermute | solution.py:485
  239.5 34.6 %collective-permute-start.24 = (bf16[48,4224]{1,0:T(8,128)(2,1)}, bf16[48,4224]{1,0:T(8,128)(2,1)S(1)}, u32[]{:S(2)}, u32[]{:S(2)}) collective-permute-start(bf16[48,4224]{1,0:T(8,128)(2,1)} %get-tuple-element.103), channel_id=1, source_target_pairs={{0,24},{8,16},{16,8},{24,0},{1,25},{9,17},{17,9},{25,1},{2,26},{10... | collective-permute-start | bytes 1216520 | tf_op jit(solution)/shard_map/ppermute | solution.py:482
  240.9 33.2 %collective-permute-start.25 = (bf16[48,4224]{1,0:T(8,128)(2,1)}, bf16[48,4224]{1,0:T(8,128)(2,1)S(1)}, u32[]{:S(2)}, u32[]{:S(2)}) collective-permute-start(bf16[48,4224]{1,0:T(8,128)(2,1)} %get-tuple-element.104), channel_id=1, source_target_pairs={{0,8},{8,0},{16,24},{24,16},{1,9},{9,1},{17,25},{25,17},{2,10},{10... | collective-permute-start | bytes 1216520 | tf_op jit(solution)/shard_map/ppermute | solution.py:482
  242.5 31.6 %collective-permute-start.26 = (bf16[48,4224]{1,0:T(8,128)(2,1)}, bf16[48,4224]{1,0:T(8,128)(2,1)S(1)}, u32[]{:S(2)}, u32[]{:S(2)}) collective-permute-start(bf16[48,4224]{1,0:T(8,128)(2,1)} %get-tuple-element.105), channel_id=1, source_target_pairs={{0,16},{8,24},{16,0},{24,8},{1,17},{9,25},{17,1},{25,9},{2,18},{10... | collective-permute-start | bytes 1216520 | tf_op jit(solution)/shard_map/ppermute | solution.py:482
  274.0 0.8 copy-start.23
  274.1 0.9 copy-start.24
  274.1 1.0 copy-start.25
  274.1 1.2 copy-start.13
  278.2 23.8 %collective-permute-start.29 = (bf16[48,4224]{1,0:T(8,128)(2,1)}, bf16[48,4224]{1,0:T(8,128)(2,1)S(1)}, u32[]{:S(2)}, u32[]{:S(2)}) collective-permute-start(bf16[48,4224]{1,0:T(8,128)(2,1)} %get-tuple-element.116), channel_id=1, source_target_pairs={{0,1},{1,2},{2,3},{3,0},{4,5},{5,6},{6,7},{7,4},{8,9},{9,10},{10,1... | collective-permute-start | bytes 1216520 | tf_op jit(solution)/shard_map/ppermute | solution.py:479
  278.5 23.4 %collective-permute-start.27 = (bf16[48,4224]{1,0:T(8,128)(2,1)}, bf16[48,4224]{1,0:T(8,128)(2,1)S(1)}, u32[]{:S(2)}, u32[]{:S(2)}) collective-permute-start(bf16[48,4224]{1,0:T(8,128)(2,1)} %get-tuple-element.116), channel_id=1, source_target_pairs={{0,0},{1,3},{2,2},{3,1},{4,4},{5,7},{6,6},{7,5},{8,8},{9,11},{10,1... | collective-permute-start | bytes 1216520 | tf_op jit(solution)/shard_map/ppermute | solution.py:479
  280.2 21.8 %collective-permute-start.30 = (bf16[48,4224]{1,0:T(8,128)(2,1)}, bf16[48,4224]{1,0:T(8,128)(2,1)S(1)}, u32[]{:S(2)}, u32[]{:S(2)}) collective-permute-start(bf16[48,4224]{1,0:T(8,128)(2,1)} %get-tuple-element.117), channel_id=1, source_target_pairs={{0,5},{1,6},{2,7},{3,4},{4,1},{5,2},{6,3},{7,0},{8,13},{9,14},{10,... | collective-permute-start | bytes 1216520 | tf_op jit(solution)/shard_map/ppermute | solution.py:479
  281.8 20.2 %collective-permute-start.28 = (bf16[48,4224]{1,0:T(8,128)(2,1)}, bf16[48,4224]{1,0:T(8,128)(2,1)S(1)}, u32[]{:S(2)}, u32[]{:S(2)}) collective-permute-start(bf16[48,4224]{1,0:T(8,128)(2,1)} %get-tuple-element.117), channel_id=1, source_target_pairs={{0,4},{1,7},{2,6},{3,5},{4,0},{5,3},{6,2},{7,1},{8,12},{9,15},{10,... | collective-permute-start | bytes 1216520 | tf_op jit(solution)/shard_map/ppermute | solution.py:479
  301.9 0.8 copy-start.18
  302.0 0.9 copy-start.19
  302.0 1.0 copy-start.20
  302.0 1.1 copy-start.21
